TPU v7x, 32 devices: a whole 2x2x4 slice. The times are simulated.
32 devices in a mesh: dp: 4 (over x, core), mp: 8 (over z, y).
Axes of the slice: x: 2, y: 2, z: 4, core: 2. Of those that a mesh axis runs over, the one named last changes fastest.
Arguments:
- hidden: bfloat16 [2048, 4096], P('dp'), may hold values from -170 to 170
- encoded: bfloat16 [32, 114688], P('dp'), may hold values from -4 to 4
- neighbours: int32 [32, 2], P('dp'), may hold values from 0 to 31, as said below
- w_query: bfloat16 [4096, 4096], P(None, 'mp'), as said below
- w_key: bfloat16 [896, 4096], P(None, 'mp'), as said below
- w_value: bfloat16 [896, 4096], P(None, 'mp'), may hold values from -0.1875 to 0.1875
- w_out: bfloat16 [4096, 4096], P('mp'), may hold values from -0.125 to 0.125
- cotangent: bfloat16 [2048, 4096], P('dp'), may hold values from -16 to 16
Outputs:
- attended: bfloat16 [2048, 4096], P('dp', 'mp')
- grad_hidden: bfloat16 [2048, 4096], P('dp', 'mp')
- grad_encoded: bfloat16 [32, 114688], P('dp', 'mp')
Inputs may be any that keep to these rules, and one draw needn't show every extreme that they name: `neighbours`: an id is owner * 8 + slot: the neighbour is row slot of the rows of encoded held by dp index owner. Of the 16 ids of one index of dp, at most 4 name one owner; one owner, the same for every index, is named exactly 4 times by every index of dp. `w_query`: entries scaled by the inverse square root of 4096. `w_key`: entries scaled by the inverse square root of 896, or smaller.
All inputs are finite; a program needn't handle non-finite values.
Results may differ from a plain program's by a relative error of at most 0.0065.
The roundings to bfloat16 on the way count: a program that leaves them out, or rounds other values in their place, can miss the bound.
Values may be sent and summed in bfloat16 or wider, within the bound.
A program may use at most 128 MiB of HBM per device.

v0:
```python
import math

import jax
import jax.numpy as jnp
from jax import lax
from jax.sharding import PartitionSpec as P

DH = 128


def shards(hidden, encoded, neighbours, w_query, w_key, w_value, w_out, cotangent):
    tok_rows = hidden.shape[0]
    owners = lax.axis_size("dp")
    blocks = neighbours.shape[0]
    per_block = neighbours.shape[1]
    requests = blocks * per_block
    capacity = requests // 4
    block_len = tok_rows // blocks
    stored = encoded.shape[0]
    enc_width = w_key.shape[0]
    seg_len = encoded.shape[1] // enc_width
    head_cols = w_query.shape[1]
    head_dim = DH
    heads_here = head_cols // head_dim
    inv_root = 1.0 / math.sqrt(head_dim)
    flat_ids = neighbours.reshape(requests)
    owner_of = flat_ids // stored
    slot_of = flat_ids % stored
    owner_mask = (owner_of[:, None] == jnp.arange(owners)[None, :]).astype(jnp.int32)
    position = jnp.sum(jnp.cumsum(owner_mask, axis=0) * owner_mask, axis=1) - 1
    target = owner_of * capacity + position
    placed = target[:, None] == jnp.arange(owners * capacity)[None, :]
    send_ids = (jnp.sum(jnp.where(placed, slot_of[:, None] + 1, 0), axis=0) - 1).reshape(
        owners, capacity
    )
    w_pair = jnp.concatenate([w_key, w_value], axis=1)
    queries = jnp.dot(hidden, w_query, preferred_element_type=jnp.float32).astype(jnp.bfloat16)
    ids_piece = lax.all_to_all(send_ids, "dp", split_axis=0, concat_axis=0, tiled=True)
    gathered = jnp.take(encoded, jnp.maximum(ids_piece, 0), axis=0)
    arrived = lax.all_to_all(gathered, "dp", split_axis=0, concat_axis=0, tiled=True)
    arrived = arrived.reshape(owners * capacity, arrived.shape[-1])
    picked = jnp.take(arrived, target, axis=0)
    fetched = jnp.dot(
        picked.reshape(requests * seg_len, enc_width), w_pair, preferred_element_type=jnp.float32
    )
    fetched = fetched.astype(jnp.bfloat16).reshape(requests, seg_len, 2 * head_cols)
    keys_all = fetched.reshape(blocks, per_block * seg_len, 2, heads_here, head_dim)
    ctx_keys = keys_all[:, :, 0]
    ctx_values = keys_all[:, :, 1]
    q_blocks = queries.reshape(blocks, block_len, heads_here, head_dim)
    scores = (
        jnp.einsum("cqhd,ckhd->chqk", q_blocks, ctx_keys, preferred_element_type=jnp.float32)
        * inv_root
    )
    row_max = jnp.max(scores, axis=-1, keepdims=True)
    exp_terms = jnp.exp(scores - row_max)
    prob_full = exp_terms / jnp.sum(exp_terms, axis=-1, keepdims=True)
    prob_half = prob_full.astype(jnp.bfloat16)
    attn_out = jnp.einsum(
        "chqk,ckhd->cqhd", prob_half, ctx_values, preferred_element_type=jnp.float32
    ).astype(jnp.bfloat16)
    attn_flat = attn_out.reshape(tok_rows, head_cols)
    partial_value = jnp.dot(attn_flat, w_out, preferred_element_type=jnp.float32)
    attended = lax.psum_scatter(partial_value, "mp", scatter_dimension=1, tiled=True).astype(
        jnp.bfloat16
    )
    grad_attn = lax.dot_general(
        cotangent, w_out, (((1,), (1,)), ((), ())), preferred_element_type=jnp.float32
    ).astype(jnp.bfloat16)
    grad_blocks = grad_attn.reshape(blocks, block_len, heads_here, head_dim)
    grad_prob = jnp.einsum(
        "cqhd,ckhd->chqk", grad_blocks, ctx_values, preferred_element_type=jnp.float32
    )
    grad_values = jnp.einsum(
        "chqk,cqhd->ckhd", prob_half, grad_blocks, preferred_element_type=jnp.float32
    ).astype(jnp.bfloat16)
    grad_scores = (
        prob_full * (grad_prob - jnp.sum(prob_full * grad_prob, axis=-1, keepdims=True))
    ).astype(jnp.bfloat16)
    grad_query = (
        jnp.einsum("chqk,ckhd->cqhd", grad_scores, ctx_keys, preferred_element_type=jnp.float32)
        * inv_root
    ).astype(jnp.bfloat16)
    grad_keys = (
        jnp.einsum("chqk,cqhd->ckhd", grad_scores, q_blocks, preferred_element_type=jnp.float32)
        * inv_root
    ).astype(jnp.bfloat16)
    grad_pair = jnp.stack([grad_keys, grad_values], axis=2).reshape(
        requests, seg_len * 2 * head_cols
    )
    outgoing = (
        jnp.zeros((owners * capacity, seg_len * 2 * head_cols), jnp.bfloat16)
        .at[target]
        .set(grad_pair)
    )
    returned = lax.all_to_all(
        outgoing.reshape(owners, capacity, seg_len * 2 * head_cols),
        "dp",
        split_axis=0,
        concat_axis=0,
        tiled=True,
    )
    gradq_flat = grad_query.reshape(tok_rows, head_cols)
    returned = returned.reshape(owners * capacity, seg_len * 2 * head_cols)
    slot_hits = (jnp.arange(stored)[:, None] == ids_piece.reshape(1, owners * capacity)).astype(
        jnp.bfloat16
    )
    grad_stored = jnp.dot(slot_hits, returned, preferred_element_type=jnp.float32).astype(
        jnp.bfloat16
    )
    grad_stored = grad_stored.reshape(stored * seg_len, 2 * head_cols)
    enc_terms = lax.dot_general(
        grad_stored, w_pair, (((1,), (1,)), ((), ())), preferred_element_type=jnp.float32
    )
    enc_terms = enc_terms.reshape(stored, seg_len * enc_width)
    grad_terms = lax.dot_general(
        gradq_flat, w_query, (((1,), (1,)), ((), ())), preferred_element_type=jnp.float32
    )
    grad_hidden, grad_encoded = (
        lax.psum_scatter(grad_terms, "mp", scatter_dimension=1, tiled=True),
        lax.psum_scatter(enc_terms, "mp", scatter_dimension=1, tiled=True),
    )
    return (attended, grad_hidden.astype(jnp.bfloat16), grad_encoded.astype(jnp.bfloat16))


def solution(mesh):
    placed = (
        P("dp", None),
        P("dp", None),
        P("dp", None),
        P(None, "mp"),
        P(None, "mp"),
        P(None, "mp"),
        P("mp", None),
        P("dp", None),
    )
    return jax.shard_map(
        shards,
        mesh=mesh,
        in_specs=placed,
        out_specs=(P("dp", "mp"), P("dp", "mp"), P("dp", "mp")),
        check_vma=False,
    )
```

profile of v0, /device:TPU:0, one launch (start us, length us, event | category | flops | bytes accessed | tf_op | source)
XLA Modules:
  0.0 910.0 jit_solution(17962865527137505000)
XLA Ops:
  52.7 27.0 %all-to-all-done.1 = bf16[4,4,114688]{2,1,0:T(4,128)(2,1)} async-done(((bf16[4,4,114688]{2,1,0:T(4,128)(2,1)}), bf16[4,4,114688]{2,1,0:T(4,128)(2,1)}, u32[]{:S(2)}, u32[]{:S(2)}) %all-to-all-start.1) | async-done | bytes 3670048 | tf_op jit(solution)/shard_map/all_to_all | solution.py:40
  83.4 10.3 %gather_fusion.1 = bf16[16,114688]{1,0:T(8,128)(2,1)} fusion(bf16[16,114688]{1,0:T(8,128)(2,1)} %reshape.233, s32[1024]{0:T(1024)S(1)} %pad_clamp_fusion), kind=kCustom, calls=%fused_computation.1 | custom fusion | bytes 7340096 | tf_op jit(solution)/shard_map/jit(_take)/gather | solution.py:42
  98.3 9.2 %convolution_convert_fusion.1 = bf16[2048,1024]{1,0:T(8,128)(2,1)} fusion(bf16[896,1024]{1,0:T(8,128)(2,1)} %copy-done.9, bf16[2048,896]{1,0:T(8,128)(2,1)} %gather.12, pred[2048]{0:T(1024)(128)(4,1)S(1)} %broadcast_bitcast_fusion), kind=kOutput, calls=%fused_computation.8 | convolution fusion | flops 3762028544 | bytes 9701376 | tf_op jit(solution)/shard_map/dot_general | solution.py:43
  153.7 280.3 %while.1 = (s32[]{:T(128)}, bf16[16,131072]{1,0:T(8,128)(2,1)}, s32[16]{0:T(128)S(1)}, bf16[16,131072]{1,0:T(8,128)(2,1)}, s32[]{:T(128)}, /*index=5*/s32[2]{0:T(128)S(1)}, s32[1]{0:T(128)}, s32[]{:T(128)}) while((s32[]{:T(128)}, bf16[16,131072]{1,0:T(8,128)(2,1)}, s32[16]{0:T(128)S(1)}, bf16[16,131072]{1,0:T(8,128)(2,1)}, s32[]{:T(128)}, ...), condition=%wide.while_cond, body=%wide.while_body.sunk | while | flops 131083 | bytes 1310855 | solution.py:94
  160.3 11.0 %dynamic-update-slice.7 = bf16[16,131072]{1,0:T(8,128)(2,1)} dynamic-update-slice(bf16[16,131072]{1,0:T(8,128)(2,1)} %get-tuple-element.65, bf16[1,131072]{1,0:T(2,128)(2,1)S(1)} %broadcast_select_fusion.3, s32[]{:T(128)} %bitcast.68, s32[]{:T(128)} %constant.68.clone.1..sunk) | dynamic-update-slice | bytes 524292 | tf_op jit(solution)/shard_map/scatter
  177.8 11.0 %dynamic-update-slice.7 = bf16[16,131072]{1,0:T(8,128)(2,1)} dynamic-update-slice(bf16[16,131072]{1,0:T(8,128)(2,1)} %get-tuple-element.65, bf16[1,131072]{1,0:T(2,128)(2,1)S(1)} %broadcast_select_fusion.3, s32[]{:T(128)} %bitcast.68, s32[]{:T(128)} %constant.68.clone.1..sunk) | dynamic-update-slice | bytes 524292 | tf_op jit(solution)/shard_map/scatter
  195.3 11.0 %dynamic-update-slice.7 = bf16[16,131072]{1,0:T(8,128)(2,1)} dynamic-update-slice(bf16[16,131072]{1,0:T(8,128)(2,1)} %get-tuple-element.65, bf16[1,131072]{1,0:T(2,128)(2,1)S(1)} %broadcast_select_fusion.3, s32[]{:T(128)} %bitcast.68, s32[]{:T(128)} %constant.68.clone.1..sunk) | dynamic-update-slice | bytes 524292 | tf_op jit(solution)/shard_map/scatter
  212.8 11.0 %dynamic-update-slice.7 = bf16[16,131072]{1,0:T(8,128)(2,1)} dynamic-update-slice(bf16[16,131072]{1,0:T(8,128)(2,1)} %get-tuple-element.65, bf16[1,131072]{1,0:T(2,128)(2,1)S(1)} %broadcast_select_fusion.3, s32[]{:T(128)} %bitcast.68, s32[]{:T(128)} %constant.68.clone.1..sunk) | dynamic-update-slice | bytes 524292 | tf_op jit(solution)/shard_map/scatter
  230.4 11.0 %dynamic-update-slice.7 = bf16[16,131072]{1,0:T(8,128)(2,1)} dynamic-update-slice(bf16[16,131072]{1,0:T(8,128)(2,1)} %get-tuple-element.65, bf16[1,131072]{1,0:T(2,128)(2,1)S(1)} %broadcast_select_fusion.3, s32[]{:T(128)} %bitcast.68, s32[]{:T(128)} %constant.68.clone.1..sunk) | dynamic-update-slice | bytes 524292 | tf_op jit(solution)/shard_map/scatter
  247.9 11.0 %dynamic-update-slice.7 = bf16[16,131072]{1,0:T(8,128)(2,1)} dynamic-update-slice(bf16[16,131072]{1,0:T(8,128)(2,1)} %get-tuple-element.65, bf16[1,131072]{1,0:T(2,128)(2,1)S(1)} %broadcast_select_fusion.3, s32[]{:T(128)} %bitcast.68, s32[]{:T(128)} %constant.68.clone.1..sunk) | dynamic-update-slice | bytes 524292 | tf_op jit(solution)/shard_map/scatter
  265.4 11.0 %dynamic-update-slice.7 = bf16[16,131072]{1,0:T(8,128)(2,1)} dynamic-update-slice(bf16[16,131072]{1,0:T(8,128)(2,1)} %get-tuple-element.65, bf16[1,131072]{1,0:T(2,128)(2,1)S(1)} %broadcast_select_fusion.3, s32[]{:T(128)} %bitcast.68, s32[]{:T(128)} %constant.68.clone.1..sunk) | dynamic-update-slice | bytes 524292 | tf_op jit(solution)/shard_map/scatter
  282.9 11.0 %dynamic-update-slice.7 = bf16[16,131072]{1,0:T(8,128)(2,1)} dynamic-update-slice(bf16[16,131072]{1,0:T(8,128)(2,1)} %get-tuple-element.65, bf16[1,131072]{1,0:T(2,128)(2,1)S(1)} %broadcast_select_fusion.3, s32[]{:T(128)} %bitcast.68, s32[]{:T(128)} %constant.68.clone.1..sunk) | dynamic-update-slice | bytes 524292 | tf_op jit(solution)/shard_map/scatter
  300.4 11.0 %dynamic-update-slice.7 = bf16[16,131072]{1,0:T(8,128)(2,1)} dynamic-update-slice(bf16[16,131072]{1,0:T(8,128)(2,1)} %get-tuple-element.65, bf16[1,131072]{1,0:T(2,128)(2,1)S(1)} %broadcast_select_fusion.3, s32[]{:T(128)} %bitcast.68, s32[]{:T(128)} %constant.68.clone.1..sunk) | dynamic-update-slice | bytes 524292 | tf_op jit(solution)/shard_map/scatter
  317.9 11.0 %dynamic-update-slice.7 = bf16[16,131072]{1,0:T(8,128)(2,1)} dynamic-update-slice(bf16[16,131072]{1,0:T(8,128)(2,1)} %get-tuple-element.65, bf16[1,131072]{1,0:T(2,128)(2,1)S(1)} %broadcast_select_fusion.3, s32[]{:T(128)} %bitcast.68, s32[]{:T(128)} %constant.68.clone.1..sunk) | dynamic-update-slice | bytes 524292 | tf_op jit(solution)/shard_map/scatter
  335.4 11.0 %dynamic-update-slice.7 = bf16[16,131072]{1,0:T(8,128)(2,1)} dynamic-update-slice(bf16[16,131072]{1,0:T(8,128)(2,1)} %get-tuple-element.65, bf16[1,131072]{1,0:T(2,128)(2,1)S(1)} %broadcast_select_fusion.3, s32[]{:T(128)} %bitcast.68, s32[]{:T(128)} %constant.68.clone.1..sunk) | dynamic-update-slice | bytes 524292 | tf_op jit(solution)/shard_map/scatter
  353.0 11.0 %dynamic-update-slice.7 = bf16[16,131072]{1,0:T(8,128)(2,1)} dynamic-update-slice(bf16[16,131072]{1,0:T(8,128)(2,1)} %get-tuple-element.65, bf16[1,131072]{1,0:T(2,128)(2,1)S(1)} %broadcast_select_fusion.3, s32[]{:T(128)} %bitcast.68, s32[]{:T(128)} %constant.68.clone.1..sunk) | dynamic-update-slice | bytes 524292 | tf_op jit(solution)/shard_map/scatter
  370.5 11.0 %dynamic-update-slice.7 = bf16[16,131072]{1,0:T(8,128)(2,1)} dynamic-update-slice(bf16[16,131072]{1,0:T(8,128)(2,1)} %get-tuple-element.65, bf16[1,131072]{1,0:T(2,128)(2,1)S(1)} %broadcast_select_fusion.3, s32[]{:T(128)} %bitcast.68, s32[]{:T(128)} %constant.68.clone.1..sunk) | dynamic-update-slice | bytes 524292 | tf_op jit(solution)/shard_map/scatter
  388.0 11.0 %dynamic-update-slice.7 = bf16[16,131072]{1,0:T(8,128)(2,1)} dynamic-update-slice(bf16[16,131072]{1,0:T(8,128)(2,1)} %get-tuple-element.65, bf16[1,131072]{1,0:T(2,128)(2,1)S(1)} %broadcast_select_fusion.3, s32[]{:T(128)} %bitcast.68, s32[]{:T(128)} %constant.68.clone.1..sunk) | dynamic-update-slice | bytes 524292 | tf_op jit(solution)/shard_map/scatter
  405.5 11.0 %dynamic-update-slice.7 = bf16[16,131072]{1,0:T(8,128)(2,1)} dynamic-update-slice(bf16[16,131072]{1,0:T(8,128)(2,1)} %get-tuple-element.65, bf16[1,131072]{1,0:T(2,128)(2,1)S(1)} %broadcast_select_fusion.3, s32[]{:T(128)} %bitcast.68, s32[]{:T(128)} %constant.68.clone.1..sunk) | dynamic-update-slice | bytes 524292 | tf_op jit(solution)/shard_map/scatter
  423.1 11.0 %dynamic-update-slice.7 = bf16[16,131072]{1,0:T(8,128)(2,1)} dynamic-update-slice(bf16[16,131072]{1,0:T(8,128)(2,1)} %get-tuple-element.65, bf16[1,131072]{1,0:T(2,128)(2,1)S(1)} %broadcast_select_fusion.3, s32[]{:T(128)} %bitcast.68, s32[]{:T(128)} %constant.68.clone.1..sunk) | dynamic-update-slice | bytes 524292 | tf_op jit(solution)/shard_map/scatter
  443.5 48.1 %all-to-all-done.2 = bf16[4,4,131072]{2,1,0:T(4,128)(2,1)} async-done(((bf16[4,4,131072]{2,1,0:T(4,128)(2,1)}), bf16[4,4,131072]{2,1,0:T(4,128)(2,1)}, u32[]{:S(2)}, u32[]{:S(2)}) %all-to-all-start.2) | async-done | bytes 4194336 | tf_op jit(solution)/shard_map/all_to_all | solution.py:96
  537.8 58.1 %reduce-scatter.8.cloned.1.call-done = f32[8,14336]{1,0:T(8,128)} async-done(((f32[8,114688]{1,0:T(8,128)}), f32[8,14336]{1,0:T(8,128)}) %reduce-scatter.8.cloned.1.call-update) | async-done | bytes 458768 | tf_op jit(solution)/shard_map/reduce_scatter | solution.py:121
  597.7 151.0 %reduce-scatter.4.cloned.1.call-done = f32[512,512]{1,0:T(8,128)} async-done(((f32[512,4096]{1,0:T(8,128)}), f32[512,512]{1,0:T(8,128)}) %reduce-scatter.4.cloned.1.call-update) | async-done | bytes 1048592 | tf_op jit(solution)/shard_map/reduce_scatter | solution.py:64
  750.8 150.4 %reduce-scatter.6.cloned.1.call-done = f32[512,512]{1,0:T(8,128)} async-done(((f32[512,4096]{1,0:T(8,128)}), f32[512,512]{1,0:T(8,128)}) %reduce-scatter.6.cloned.1.call-update) | async-done | bytes 1048592 | tf_op jit(solution)/shard_map/reduce_scatter | solution.py:120
  (138 shorter events, 265.9 us)
Async XLA Ops:
  7.2 10.5 %copy-start = (bf16[8,114688]{1,0:T(8,128)(2,1)S(1)}, bf16[8,114688]{1,0:T(8,128)(2,1)}, u32[]{:S(2)}) copy-start(bf16[8,114688]{1,0:T(8,128)(2,1)} %param.9) | copy-start | bytes 5505028
  32.1 47.5 %all-to-all-start.1 = ((bf16[4,4,114688]{2,1,0:T(4,128)(2,1)}), bf16[4,4,114688]{2,1,0:T(4,128)(2,1)}, u32[]{:S(2)}, u32[]{:S(2)}) async-start(bf16[4,4,114688]{2,1,0:T(4,128)(2,1)} %broadcast_select_fusion.1), calls=%async_computation.1 | async-start | bytes 7340032 | tf_op jit(solution)/shard_map/all_to_all | solution.py:40
  43.1 8.0 copy-start.7
  49.7 1.4 copy-start.8
  51.3 1.3 copy-start.9
  119.2 1.4 copy-start.4
  120.6 2.0 copy-start.2
  129.6 3.3 copy-start.3
  133.7 1.6 copy-start.6
  151.5 2.3 copy-start.10
  438.5 53.1 %all-to-all-start.2 = ((bf16[4,4,131072]{2,1,0:T(4,128)(2,1)}), bf16[4,4,131072]{2,1,0:T(4,128)(2,1)}, u32[]{:S(2)}, u32[]{:S(2)}) async-start(bf16[4,4,131072]{2,1,0:T(4,128)(2,1)} %reshape.240), calls=%async_computation.4 | async-start | bytes 8388608 | tf_op jit(solution)/shard_map/all_to_all | solution.py:96
  443.4 152.6 %reduce-scatter.8.cloned.1.call-start = ((), (), s32[]{:S(2)}) async-start(), calls=%async_computation.8 | async-start | bytes 4128768 | tf_op jit(solution)/shard_map/reduce_scatter | solution.py:121
  514.6 234.1 %reduce-scatter.4.cloned.1.call-start = ((), (), s32[]{:S(2)}) async-start(), calls=%async_computation.6 | async-start | bytes 9437184 | tf_op jit(solution)/shard_map/reduce_scatter | solution.py:64
  529.2 372.0 %reduce-scatter.6.cloned.1.call-start = ((), (), s32[]{:S(2)}) async-start(), calls=%async_computation.7 | async-start | bytes 9437184 | tf_op jit(solution)/shard_map/reduce_scatter | solution.py:120
  529.3 2.9 copy-start.5
  537.8 365.5 %copy-start.1 = (bf16[8,114688]{1,0:T(8,128)(2,1)S(1)}, bf16[8,114688]{1,0:T(8,128)(2,1)}, u32[]{:S(2)}) copy-start(bf16[8,114688]{1,0:T(8,128)(2,1)} %param.9) | copy-start | bytes 5505028
Sparse Core Ops, SparseCore 0:
  514.7 81.1 reduce-scatter.7
  599.6 149.1 reduce-scatter.3
  752.8 148.3 reduce-scatter.5
where the time goes:
time: 920 us; the launch traced here: 910 us
  waiting for transfers between devices  435 us (47%)
  local copies, waits for them, and re-layouts  265 us (29%)
  other arithmetic  113 us (12%)
  matrix products  65.8 us (7%)
  between operations  14.2 us (2%)
  starting transfers between devices  10.1 us (1%)
    scatter x32, local copies, waits for them, and re-layouts  185 us
    reduce_scatter x1, waiting for transfers between devices, shards(): lax.psum_scatter(partial_value, 'mp', scatter_dimension=1, tiled=True)  151 us
    reduce_scatter x1, waiting for transfers between devices, shards(): lax.psum_scatter(grad_terms, 'mp', scatter_dimension=1, tiled=True)  150 us
    scatter x32, other arithmetic  95.2 us
    reduce_scatter x1, waiting for transfers between devices, shards(): lax.psum_scatter(enc_terms, 'mp', scatter_dimension=1, tiled=True)  58.1 us
    all_to_all x1, waiting for transfers between devices, shards(): lax.all_to_all(outgoing.reshape(owners, capacity, seg_len * 2 * head_cols...  48.1 us
    all_to_all x1, waiting for transfers between devices, shards(): lax.all_to_all(gathered, 'dp', split_axis=0, concat_axis=0, tiled=True)  27 us
  transfers between devices with their start and end apart: 5, of which 5 were waited for; matrix products, arithmetic and copies ran while one was open for 4% of the time, Pallas kernels for 0%

commit v1 on v0

v1 whole, which is shorter than its diff:
```python
import functools
import math

import jax
import jax.numpy as jnp
from jax import lax
from jax.experimental import pallas as pl
from jax.experimental.pallas import tpu as pltpu
from jax.sharding import PartitionSpec as P

DH = 128
VMEM_BYTES = 48 * 1024 * 1024


def dot(a, b, contract):
    return lax.dot_general(a, b, ((contract[:1], contract[1:]), ((), ())), preferred_element_type=jnp.float32)


def attention_kernel(per_block, ids, target, q_ref, ga_ref, *refs):
    kv_refs = refs[:per_block]
    attn_ref, gq_ref, out_ref = refs[per_block:]
    step = pl.program_id(0)
    cols = q_ref.shape[1]
    seg = kv_refs[0].shape[1]
    inv_root = 1.0 / math.sqrt(DH)

    if out_ref.shape[0] > target.shape[0]:
        @pl.when(step == 0)
        def _():
            out_ref[...] = jnp.zeros_like(out_ref)

    for h in range(cols // DH):
        at = h * DH
        q = q_ref[:, at:at + DH]
        ga = ga_ref[:, at:at + DH]
        k = jnp.concatenate([r[0, :, at:at + DH] for r in kv_refs], axis=0)
        v = jnp.concatenate([r[0, :, cols + at:cols + at + DH] for r in kv_refs], axis=0)
        scores = dot(q, k, (1, 1)) * inv_root
        grad_prob = dot(ga, v, (1, 1))
        terms = jnp.exp(scores - jnp.max(scores, axis=-1, keepdims=True))
        prob = terms / jnp.sum(terms, axis=-1, keepdims=True)
        half = prob.astype(jnp.bfloat16)
        attn_ref[:, at:at + DH] = dot(half, v, (1, 0)).astype(jnp.bfloat16)
        grad_v = dot(half, ga, (0, 0)).astype(jnp.bfloat16)
        gs = (prob * (grad_prob - jnp.sum(prob * grad_prob, axis=-1, keepdims=True))).astype(jnp.bfloat16)
        gq_ref[:, at:at + DH] = (dot(gs, k, (1, 0)) * inv_root).astype(jnp.bfloat16)
        grad_k = (dot(gs, q, (0, 0)) * inv_root).astype(jnp.bfloat16)
        for j in range(per_block):
            slot = target[step * per_block + j]
            out_ref[slot, :, at:at + DH] = grad_k[j * seg:(j + 1) * seg]
            out_ref[slot, :, cols + at:cols + at + DH] = grad_v[j * seg:(j + 1) * seg]


def attention(ids, target, queries, grad_attn, kv, blocks, slots):
    per_block = ids.shape[0] // blocks
    tok, cols = queries.shape
    block_len = tok // blocks
    seg = kv.shape[1]
    row = pl.BlockSpec((block_len, cols), lambda c, ids, tg: (c, 0))

    def kv_spec(j):
        return pl.BlockSpec((1, seg, 2 * cols), lambda c, ids, tg: (ids[c * per_block + j], 0, 0))

    return pl.pallas_call(
        functools.partial(attention_kernel, per_block),
        grid_spec=pltpu.PrefetchScalarGridSpec(
            num_scalar_prefetch=2,
            grid=(blocks,),
            in_specs=[row, row] + [kv_spec(j) for j in range(per_block)],
            out_specs=[row, row, pl.BlockSpec((slots, seg, 2 * cols), lambda c, ids, tg: (0, 0, 0))],
        ),
        out_shape=[
            jax.ShapeDtypeStruct((tok, cols), jnp.bfloat16),
            jax.ShapeDtypeStruct((tok, cols), jnp.bfloat16),
            jax.ShapeDtypeStruct((slots, seg, 2 * cols), jnp.bfloat16),
        ],
        compiler_params=pltpu.CompilerParams(vmem_limit_bytes=VMEM_BYTES),
        name="attention",
    )(ids, target, queries, grad_attn, *([kv] * per_block))


def sum_kernel(count, ids, ret_ref, out_ref, acc):
    acc[...] = jnp.zeros_like(acc)

    @pl.loop(0, count)
    def _(i):
        slot = ids[i]

        @pl.when(slot >= 0)
        def _():
            acc[slot] = acc[slot] + ret_ref[i].astype(jnp.float32)

    out_ref[...] = acc[...].astype(jnp.bfloat16)


def sum_slots(ids, returned, stored):
    shape = (stored,) + returned.shape[1:]
    return pl.pallas_call(
        functools.partial(sum_kernel, returned.shape[0]),
        grid_spec=pltpu.PrefetchScalarGridSpec(
            num_scalar_prefetch=1,
            grid=(1,),
            in_specs=[pl.BlockSpec(returned.shape, lambda i, ids: (0, 0, 0))],
            out_specs=pl.BlockSpec(shape, lambda i, ids: (0, 0, 0)),
            scratch_shapes=[pltpu.VMEM(shape, jnp.float32)],
        ),
        out_shape=jax.ShapeDtypeStruct(shape, jnp.bfloat16),
        compiler_params=pltpu.CompilerParams(vmem_limit_bytes=VMEM_BYTES),
        name="sum_slots",
    )(ids, returned)


def shards(hidden, encoded, neighbours, w_query, w_key, w_value, w_out, cotangent):
    owners = lax.axis_size("dp")
    me = lax.axis_index("dp")
    blocks, per_block = neighbours.shape
    requests = blocks * per_block
    capacity = requests // 4
    stored = encoded.shape[0]
    enc_width, head_cols = w_key.shape
    seg_len = encoded.shape[1] // enc_width

    w_pair = jnp.concatenate([w_key, w_value], axis=1)
    enc_rows = encoded.reshape(stored * seg_len, enc_width)
    kv_own = jnp.dot(enc_rows, w_pair, preferred_element_type=jnp.float32).astype(jnp.bfloat16)
    kv = lax.all_gather(kv_own.reshape(stored, seg_len, 2 * head_cols), "dp", axis=0, tiled=True)
    queries = jnp.dot(hidden, w_query, preferred_element_type=jnp.float32).astype(jnp.bfloat16)
    grad_attn = dot(cotangent, w_out, (1, 1)).astype(jnp.bfloat16)

    ids = lax.all_gather(neighbours.reshape(requests), "dp", axis=0)
    owner_of = ids // stored
    slot_of = ids % stored
    same = owner_of[:, :, None] == owner_of[:, None, :]
    before = jnp.arange(requests)[:, None] > jnp.arange(requests)[None, :]
    position = jnp.sum((same & before[None]).astype(jnp.int32), axis=2)
    wanted = (owner_of == me)[:, :, None] & (position[:, :, None] == jnp.arange(capacity)[None, None, :])
    my_slots = (jnp.sum(jnp.where(wanted, slot_of[:, :, None] + 1, 0), axis=1) - 1).reshape(owners * capacity)
    flat_ids = neighbours.reshape(requests)
    flat_owner = flat_ids // stored
    mine = flat_owner[:, None] == flat_owner[None, :]
    target = flat_owner * capacity + jnp.sum((mine & before).astype(jnp.int32), axis=1)

    attn, grad_query, outgoing = attention(
        flat_ids, target, queries, grad_attn, kv, blocks, owners * capacity
    )
    returned = lax.all_to_all(outgoing, "dp", split_axis=0, concat_axis=0, tiled=True)
    partial_value = jnp.dot(attn, w_out, preferred_element_type=jnp.float32).astype(jnp.bfloat16)
    attended = lax.psum_scatter(partial_value, "mp", scatter_dimension=1, tiled=True)
    grad_terms = dot(grad_query, w_query, (1, 1)).astype(jnp.bfloat16)
    grad_hidden = lax.psum_scatter(grad_terms, "mp", scatter_dimension=1, tiled=True)
    grad_stored = sum_slots(my_slots, returned, stored)
    enc_terms = dot(grad_stored.reshape(stored * seg_len, 2 * head_cols), w_pair, (1, 1))
    enc_terms = enc_terms.astype(jnp.bfloat16).reshape(stored, seg_len, enc_width)
    grad_encoded = lax.psum_scatter(enc_terms, "mp", scatter_dimension=1, tiled=True)
    return attended, grad_hidden, grad_encoded.reshape(stored, -1)


def solution(mesh):
    placed = (
        P("dp", None),
        P("dp", None),
        P("dp", None),
        P(None, "mp"),
        P(None, "mp"),
        P(None, "mp"),
        P("mp", None),
        P("dp", None),
    )
    return jax.shard_map(
        shards,
        mesh=mesh,
        in_specs=placed,
        out_specs=(P("dp", "mp"), P("dp", "mp"), P("dp", "mp")),
        check_vma=False,
    )
```

time: 920 us -> 414 us (0.45)
  local copies, waits for them, and re-layouts: 265 us -> 5.86 us
  waiting for transfers between devices: 435 us -> 288 us
  other arithmetic: 113 us -> 0.61 us
  blocking collectives: 7.76 us -> 48.9 us
  matrix products: 65.8 us -> 28.7 us
  Pallas kernels: 0 us -> 22 us
    scatter x32 -> x0, local copies, waits for them, and re-layouts: 185 us -> none
    scatter x32 -> x0, other arithmetic: 95.2 us -> none
    all_to_all x2 -> x1, waiting for transfers between devices: 75.1 us -> 0.01 us  [shards(): lax.all_to_all(outgoing, 'dp', split_axis=0, concat_axis=0, tiled=True)]
    reduce_scatter x1, waiting for transfers between devices: 151 us -> 90.3 us  [shards(): lax.psum_scatter(partial_value, 'mp', scatter_dimension=1, tiled=True)]
    reduce_scatter x1, waiting for transfers between devices: 150 us -> 92.3 us  [shards(): lax.psum_scatter(grad_terms, 'mp', scatter_dimension=1, tiled=True)]
    all_gather x0 -> x1, waiting for transfers between devices: none -> 52.4 us  [shards(): lax.all_gather(kv_own.reshape(stored, seg_len, 2 * head_cols), 'dp', axis...]
    all_gather x0 -> x1, blocking collectives: none -> 48.9 us  [shards(): ids = lax.all_gather(neighbours.reshape(requests), 'dp', axis=0)]
    dot_general x12 -> x5, matrix products: 60 us -> 22.8 us  [the longest x3 12.6 us: dot(): lax.dot_general(a, b, ((contract[:1], contract[1:]), ((), ())), preferred...]
  transfers between devices with their start and end apart: 5 -> 5, of which waited for: 5 -> 4; matrix products, arithmetic and copies ran while one was open for 4% -> 6% of each run, Pallas kernels for 0% -> 0%
where the time goes in v1:
time: 414 us; the launch traced here: 413 us
  waiting for transfers between devices  288 us (70%)
  blocking collectives  48.9 us (12%)
  matrix products  28.7 us (7%)
  Pallas kernels  22 us (5%)
  between operations  13.9 us (3%)
  local copies, waits for them, and re-layouts  5.86 us (1%)
  starting transfers between devices  5.18 us (1%)
    reduce_scatter x1, waiting for transfers between devices, shards(): lax.psum_scatter(grad_terms, 'mp', scatter_dimension=1, tiled=True)  92.3 us
    reduce_scatter x1, waiting for transfers between devices, shards(): lax.psum_scatter(partial_value, 'mp', scatter_dimension=1, tiled=True)  90.3 us
    reduce_scatter x1, waiting for transfers between devices, shards(): lax.psum_scatter(enc_terms, 'mp', scatter_dimension=1, tiled=True)  53 us
    all_gather x1, waiting for transfers between devices, shards(): lax.all_gather(kv_own.reshape(stored, seg_len, 2 * head_cols), 'dp', axis...  52.4 us
    all_gather x1, blocking collectives, shards(): ids = lax.all_gather(neighbours.reshape(requests), 'dp', axis=0)  48.9 us
    pallas_call x1, Pallas kernels, attention(): pl.pallas_call(functools.partial(attention_kernel, per_block), grid_spec=...  17.9 us
    dot_general x3, matrix products, dot(): lax.dot_general(a, b, ((contract[:1], contract[1:]), ((), ())), preferred...  12.6 us
  transfers between devices with their start and end apart: 5, of which 4 were waited for; matrix products, arithmetic and copies ran while one was open for 6% of the time, Pallas kernels for 0%

profile of v1, /device:TPU:0, one launch (start us, length us, event | category | flops | bytes accessed | tf_op | source)
XLA Modules:
  0.0 413.2 jit_solution(10664454494251658490)
XLA Ops:
  7.2 2.4 reshape.105
  9.6 0.1 constant_dynamic-update-slice_fusion.1
  9.8 1.3 constant_dynamic-update-slice_fusion
  11.1 3.7 convolution_convert_fusion.2
  14.8 0.1 copy.17
  15.0 0.2 convert_reduce_fusion.1
  15.2 5.9 %convolution_convert_fusion.5.q_ref = bf16[512,512]{1,0:T(8,128)(2,1)S(1)} fusion(bf16[512,4096]{1,0:T(8,128)(2,1)} %param.8, bf16[4096,512]{1,0:T(8,128)(2,1)} %param.11), kind=kOutput, calls=%fused_computation.5 | convolution fusion | flops 2147745792 | bytes 8912896 | tf_op jit(solution)/shard_map/dot_general | solution.py:127
  21.2 2.4 convolution_convert_fusion.4.ga_ref
  23.6 52.4 %all-gather.3.cloned.1.call-done.refs_0_.refs_1_ = bf16[32,128,1024]{2,1,0:T(8,128)(2,1)} async-done(((bf16[8,128,1024]{2,1,0:T(8,128)(2,1)}), bf16[32,128,1024]{2,1,0:T(8,128)(2,1)}) %all-gather.3.cloned.1.call-update) | async-done | bytes 8388624 | tf_op jit(solution)/shard_map/all_gather | solution.py:126
  76.0 17.9 %attention.1 = (bf16[512,512]{1,0:T(8,128)(2,1)S(1)}, bf16[512,512]{1,0:T(8,128)(2,1)S(1)}, bf16[16,128,1024]{2,1,0:T(8,128)(2,1)}) custom-call(s32[16]{0:T(128)S(1)} %reshape.104.ids, s32[16]{0:T(128)S(1)} %multiply_add_fusion.target, bf16[512,512]{1,0:T(8,128)(2,1)S(1)} %convolution_convert_fusion.5.q_ref, ...), custom_call_target="tpu_custom_call" | custom-call | tf_op jit(solution)/shard_map/attention/pallas_call | solution.py:64
  93.9 4.8 %all-to-all-start = ((bf16[16,128,1024]{2,1,0:T(8,128)(2,1)}), bf16[16,128,1024]{2,1,0:T(8,128)(2,1)}, u32[]{:S(2)}, u32[]{:S(2)}) async-start(bf16[16,128,1024]{2,1,0:T(8,128)(2,1)} %get-tuple-element.8), calls=%async_computation.2 | async-start | bytes 8388608 | tf_op jit(solution)/shard_map/all_to_all | solution.py:146
  98.9 48.9 %all-gather = s32[4,1,16]{2,1,0:T(1,128)S(1)} all-gather(s32[1,1,16]{2,1,0:T(1,128)S(1)} %reshape.111), channel_id=1, replica_groups=mesh['dp'=4,'mp'=8] {'dp'}, dimensions={0}, use_global_device_ids=true | all-gather | bytes 320 | tf_op jit(solution)/shard_map/all_gather | solution.py:130
  147.8 0.2 convert_reduce_fusion
  148.0 0.1 select_reduce_fusion
  148.2 0.1 sub.18.ids
  148.3 4.1 sum_slots.1
  152.4 3.7 convolution_convert_fusion.3
  156.1 0.2 reduce-scatter.4.cloned.1.call-start
  156.3 6.5 %convolution_convert_fusion.1 = bf16[512,4096]{1,0:T(8,128)(2,1)} fusion(bf16[512,512]{1,0:T(8,128)(2,1)S(1)} %get-tuple-element.6, bf16[512,4096]{1,0:T(8,128)(2,1)} %param.14), kind=kOutput, calls=%fused_computation.1 | convolution fusion | flops 2149580800 | bytes 8912896 | tf_op jit(solution)/shard_map/dot_general | solution.py:147
  162.9 6.6 %convolution_convert_fusion = bf16[512,4096]{1,0:T(8,128)(2,1)} fusion(bf16[512,512]{1,0:T(8,128)(2,1)S(1)} %get-tuple-element.7, bf16[4096,512]{1,0:T(8,128)(2,1)} %param.11), kind=kOutput, calls=%fused_computation | convolution fusion | flops 2149580800 | bytes 8912896 | tf_op jit(solution)/shard_map/dot_general | solution.py:16
  169.5 53.0 %reduce-scatter.8.cloned.1.call-done = bf16[8,16,896]{2,1,0:T(8,128)(2,1)} async-done(((bf16[8,128,896]{2,1,0:T(8,128)(2,1)}), bf16[8,16,896]{2,1,0:T(8,128)(2,1)}) %reduce-scatter.8.cloned.1.call-update) | async-done | bytes 229392 | tf_op jit(solution)/shard_map/reduce_scatter | solution.py:154
  222.4 1.7 copy.19
  224.1 90.3 %reduce-scatter.4.cloned.1.call-done = bf16[512,512]{1,0:T(8,128)(2,1)} async-done(((bf16[512,4096]{1,0:T(8,128)(2,1)}), bf16[512,512]{1,0:T(8,128)(2,1)}) %reduce-scatter.4.cloned.1.call-update) | async-done | bytes 524304 | tf_op jit(solution)/shard_map/reduce_scatter | solution.py:148
  314.3 92.3 %reduce-scatter.6.cloned.1.call-done = bf16[512,512]{1,0:T(8,128)(2,1)} async-done(((bf16[512,4096]{1,0:T(8,128)(2,1)}), bf16[512,512]{1,0:T(8,128)(2,1)}) %reduce-scatter.6.cloned.1.call-update) | async-done | bytes 524304 | tf_op jit(solution)/shard_map/reduce_scatter | solution.py:150
  (28 shorter events, 0.4 us)
Async XLA Ops:
  7.2 2.5 copy-start
  7.2 68.8 %all-gather.3.cloned.1.call-start = ((), (), s32[]{:S(2)}) async-start(), calls=%async_computation.4 | async-start | bytes 10485760 | tf_op jit(solution)/shard_map/all_gather | solution.py:126
  11.1 3.7 copy-start.1
  11.1 3.7 copy-start.3
  15.2 6.0 %copy-start.4 = (bf16[512,4096]{1,0:T(8,128)(2,1)S(1)}, bf16[512,4096]{1,0:T(8,128)(2,1)}, u32[]{:S(2)}) copy-start(bf16[512,4096]{1,0:T(8,128)(2,1)} %param.15) | copy-start | bytes 12582916
  15.2 6.0 %copy-start.5 = (bf16[512,4096]{1,0:T(8,128)(2,1)S(1)}, bf16[512,4096]{1,0:T(8,128)(2,1)}, u32[]{:S(2)}) copy-start(bf16[512,4096]{1,0:T(8,128)(2,1)} %param.14) | copy-start | bytes 12582916
  93.9 54.4 %all-to-all-start = ((bf16[16,128,1024]{2,1,0:T(8,128)(2,1)}), bf16[16,128,1024]{2,1,0:T(8,128)(2,1)}, u32[]{:S(2)}, u32[]{:S(2)}) async-start(bf16[16,128,1024]{2,1,0:T(8,128)(2,1)} %get-tuple-element.8), calls=%async_computation.2 | async-start | bytes 8388608 | tf_op jit(solution)/shard_map/all_to_all | solution.py:146
  98.7 53.6 %copy-start.2 = (bf16[896,1024]{1,0:T(8,128)(2,1)S(1)}, bf16[896,1024]{1,0:T(8,128)(2,1)}, u32[]{:S(2)}) copy-start(bf16[896,1024]{1,0:T(8,128)(2,1)} %copy-done.1) | copy-start | bytes 5505028
  98.7 123.7 %reduce-scatter.8.cloned.1.call-start = ((), (), s32[]{:S(2)}) async-start(), calls=%async_computation.7 | async-start | bytes 2064384 | tf_op jit(solution)/shard_map/reduce_scatter | solution.py:154
  156.1 158.3 %reduce-scatter.4.cloned.1.call-start = ((), (), s32[]{:S(2)}) async-start(), calls=%async_computation.5 | async-start | bytes 4718592 | tf_op jit(solution)/shard_map/reduce_scatter | solution.py:148
  162.8 243.8 %reduce-scatter.6.cloned.1.call-start = ((), (), s32[]{:S(2)}) async-start(), calls=%async_computation.6 | async-start | bytes 4718592 | tf_op jit(solution)/shard_map/reduce_scatter | solution.py:150
Sparse Core Ops, SparseCore 0:
  15.0 60.9 all-gather.2
  156.2 66.1 reduce-scatter.7
  227.1 87.2 reduce-scatter.3
  318.4 88.1 reduce-scatter.5

commit v2 on v1

--- a/solution.py
+++ b/solution.py
@@ -110,9 +110,182 @@
     )(ids, returned)
 
 
+def ring_place(n, index):
+    return jnp.where(index % 2 == 0, index // 2, n - 1 - index // 2)
+
+
+def ring_index(n, place):
+    return jnp.where(place < n // 2, 2 * place, 2 * (n - 1 - place) + 1)
+
+
+def ring_setup(n):
+    forward = 1 - 2 * (lax.axis_index("dp") % 2)
+    place = ring_place(n, lax.axis_index("mp"))
+    ahead = ring_index(n, (place + forward + n) % n)
+    behind = ring_index(n, (place - forward + n) % n)
+
+    def chunk(step):
+        return ring_index(n, (place - forward * (1 + step) + 2 * n) % n)
+
+    return ahead, behind, chunk
+
+
+def ring_sum(n, ahead, chunk, streams):
+    def copy(stream, src, step):
+        _, buf, send_sem, recv_sem, _, _ = stream
+        return pltpu.make_async_remote_copy(
+            src_ref=src,
+            dst_ref=buf.at[step],
+            send_sem=send_sem.at[step],
+            recv_sem=recv_sem.at[step],
+            device_id={"mp": ahead},
+            device_id_type=pl.DeviceIdType.MESH,
+        )
+
+    for stream in streams:
+        part, first = stream[0], stream[4]
+        first[...] = part(chunk(0)).astype(jnp.bfloat16)
+        copy(stream, first, 0).start()
+
+    @pl.loop(1, n - 1)
+    def _(step):
+        for stream in streams:
+            part, buf = stream[:2]
+            term = part(chunk(step))
+            copy(stream, buf.at[step - 1], step - 1).wait_recv()
+            buf[step - 1] = (buf[step - 1].astype(jnp.float32) + term).astype(jnp.bfloat16)
+            copy(stream, buf.at[step - 1], step).start()
+
+    for stream in streams:
+        part, buf, _, _, first, out = stream
+        term = part(chunk(n - 1))
+        copy(stream, first, n - 2).wait_recv()
+        out[...] = (buf[n - 2].astype(jnp.float32) + term).astype(jnp.bfloat16)
+
+    @pl.loop(0, n - 1)
+    def _(step):
+        for stream in streams:
+            copy(stream, stream[4], step).wait_send()
+
+
+def exchange_kernel(
+    n, owners, attn, gq, w_out, w_query, outgoing, sent_ids,
+    att_out, hid_out, returned, returned_ids,
+    att_buf, hid_buf, att_first, hid_first, att_send, att_recv, hid_send, hid_recv,
+    data_send, data_recv, ids_send, ids_recv, local_sem,
+):
+    me = lax.axis_index("dp")
+    ahead, behind, chunk = ring_setup(n)
+    rows = outgoing.shape[0] // owners
+    width = att_out.shape[1]
+
+    barrier = pltpu.get_barrier_semaphore()
+    for device in [{"mp": ahead}, {"mp": behind}] + [{"dp": (me + d) % owners} for d in range(1, owners)]:
+        pl.semaphore_signal(barrier, inc=1, device_id=device, device_id_type=pl.DeviceIdType.MESH)
+    pl.semaphore_wait(barrier, 1 + owners)
+
+    def block(index):
+        return pl.ds(pl.multiple_of(index * rows, rows), rows)
+
+    copies = []
+    for d in range(1, owners):
+        to = (me + d) % owners
+        for src, dst, send, recv in (
+            (outgoing.at[block(to)], returned.at[block(me)], data_send, data_recv),
+            (sent_ids.at[to], returned_ids.at[me], ids_send, ids_recv),
+        ):
+            copies.append(pltpu.make_async_remote_copy(
+                src_ref=src,
+                dst_ref=dst,
+                send_sem=send.at[d - 1],
+                recv_sem=recv.at[d - 1],
+                device_id={"dp": to},
+                device_id_type=pl.DeviceIdType.MESH,
+            ))
+    local = [
+        pltpu.make_async_copy(outgoing.at[block(me)], returned.at[block(me)], local_sem.at[0]),
+        pltpu.make_async_copy(sent_ids.at[me], returned_ids.at[me], local_sem.at[1]),
+    ]
+    for copy in copies + local:
+        copy.start()
+
+    def at(index):
+        return pl.ds(pl.multiple_of(index * width, width), width)
+
+    ring_sum(n, ahead, chunk, [
+        (lambda c: dot(attn[...], w_out[:, at(c)], (1, 0)), att_buf, att_send, att_recv, att_first, att_out),
+        (lambda c: dot(gq[...], w_query[at(c), :], (1, 1)), hid_buf, hid_send, hid_recv, hid_first, hid_out),
+    ])
+    for copy in copies + local:
+        copy.wait()
+
+
+def exchange(attn, gq, w_out, w_query, outgoing, sent_ids):
+    n, owners = lax.axis_size("mp"), lax.axis_size("dp")
+    tok = attn.shape[0]
+    width = w_out.shape[1] // n
+    vmem = pl.BlockSpec(memory_space=pltpu.VMEM)
+    anywhere = pl.BlockSpec(memory_space=pl.ANY)
+    piece = jax.ShapeDtypeStruct((tok, width), jnp.bfloat16)
+    ring = pltpu.SemaphoreType.DMA((n - 1,))
+    peers = pltpu.SemaphoreType.DMA((owners - 1,))
+    return pl.pallas_call(
+        functools.partial(exchange_kernel, n, owners),
+        in_specs=[vmem] * 4 + [anywhere] * 2,
+        out_specs=[vmem, vmem, anywhere, anywhere],
+        out_shape=[
+            piece,
+            piece,
+            jax.ShapeDtypeStruct(outgoing.shape, outgoing.dtype),
+            jax.ShapeDtypeStruct(sent_ids.shape, sent_ids.dtype),
+        ],
+        scratch_shapes=[pltpu.VMEM((n - 1, tok, width), jnp.bfloat16)] * 2
+        + [pltpu.VMEM((tok, width), jnp.bfloat16)] * 2
+        + [ring] * 4
+        + [peers] * 4
+        + [pltpu.SemaphoreType.DMA((2,))],
+        compiler_params=pltpu.CompilerParams(
+            collective_id=1, has_side_effects=True, vmem_limit_bytes=VMEM_BYTES
+        ),
+        name="exchange",
+    )(attn, gq, w_out, w_query, outgoing, sent_ids)
+
+
+def encoded_kernel(n, grads, w_pair, out, buf, first, send_sem, recv_sem):
+    ahead, behind, chunk = ring_setup(n)
+    barrier = pltpu.get_barrier_semaphore()
+    for device in (ahead, behind):
+        pl.semaphore_signal(barrier, inc=1, device_id={"mp": device}, device_id_type=pl.DeviceIdType.MESH)
+    pl.semaphore_wait(barrier, 2)
+    ring_sum(n, ahead, chunk, [
+        (lambda c: dot(grads[c], w_pair[...], (1, 1)), buf, send_sem, recv_sem, first, out),
+    ])
+
+
+def encoded_sum(grads, w_pair):
+    n = lax.axis_size("mp")
+    rows, width = grads.shape[1], w_pair.shape[0]
+    vmem = pl.BlockSpec(memory_space=pltpu.VMEM)
+    return pl.pallas_call(
+        functools.partial(encoded_kernel, n),
+        in_specs=[vmem] * 2,
+        out_specs=vmem,
+        out_shape=jax.ShapeDtypeStruct((rows, width), jnp.bfloat16),
+        scratch_shapes=[
+            pltpu.VMEM((n - 1, rows, width), jnp.bfloat16),
+            pltpu.VMEM((rows, width), jnp.bfloat16),
+            pltpu.SemaphoreType.DMA((n - 1,)),
+            pltpu.SemaphoreType.DMA((n - 1,)),
+        ],
+        compiler_params=pltpu.CompilerParams(
+            collective_id=2, has_side_effects=True, vmem_limit_bytes=VMEM_BYTES
+        ),
+        name="encoded_sum",
+    )(grads, w_pair)
+
+
 def shards(hidden, encoded, neighbours, w_query, w_key, w_value, w_out, cotangent):
     owners = lax.axis_size("dp")
-    me = lax.axis_index("dp")
     blocks, per_block = neighbours.shape
     requests = blocks * per_block
     capacity = requests // 4
@@ -127,31 +300,28 @@
     queries = jnp.dot(hidden, w_query, preferred_element_type=jnp.float32).astype(jnp.bfloat16)
     grad_attn = dot(cotangent, w_out, (1, 1)).astype(jnp.bfloat16)
 
-    ids = lax.all_gather(neighbours.reshape(requests), "dp", axis=0)
-    owner_of = ids // stored
-    slot_of = ids % stored
-    same = owner_of[:, :, None] == owner_of[:, None, :]
-    before = jnp.arange(requests)[:, None] > jnp.arange(requests)[None, :]
-    position = jnp.sum((same & before[None]).astype(jnp.int32), axis=2)
-    wanted = (owner_of == me)[:, :, None] & (position[:, :, None] == jnp.arange(capacity)[None, None, :])
-    my_slots = (jnp.sum(jnp.where(wanted, slot_of[:, :, None] + 1, 0), axis=1) - 1).reshape(owners * capacity)
     flat_ids = neighbours.reshape(requests)
     flat_owner = flat_ids // stored
     mine = flat_owner[:, None] == flat_owner[None, :]
+    before = jnp.arange(requests)[:, None] > jnp.arange(requests)[None, :]
     target = flat_owner * capacity + jnp.sum((mine & before).astype(jnp.int32), axis=1)
+    placed = target[:, None] == jnp.arange(owners * capacity)[None, :]
+    sent_ids = jnp.sum(jnp.where(placed, (flat_ids % stored)[:, None] + 1, 0), axis=0) - 1
+    sent_ids = jnp.broadcast_to(sent_ids.reshape(owners, 1, capacity), (owners, 8, capacity))
+    sent_ids = jnp.pad(sent_ids, ((0, 0), (0, 0), (0, 128 - capacity)))
 
     attn, grad_query, outgoing = attention(
         flat_ids, target, queries, grad_attn, kv, blocks, owners * capacity
     )
-    returned = lax.all_to_all(outgoing, "dp", split_axis=0, concat_axis=0, tiled=True)
-    partial_value = jnp.dot(attn, w_out, preferred_element_type=jnp.float32).astype(jnp.bfloat16)
-    attended = lax.psum_scatter(partial_value, "mp", scatter_dimension=1, tiled=True)
-    grad_terms = dot(grad_query, w_query, (1, 1)).astype(jnp.bfloat16)
-    grad_hidden = lax.psum_scatter(grad_terms, "mp", scatter_dimension=1, tiled=True)
+    attended, grad_hidden, returned, returned_ids = exchange(
+        attn, grad_query, w_out, w_query, outgoing, sent_ids
+    )
+    my_slots = returned_ids[:, 0, :capacity].reshape(owners * capacity)
     grad_stored = sum_slots(my_slots, returned, stored)
-    enc_terms = dot(grad_stored.reshape(stored * seg_len, 2 * head_cols), w_pair, (1, 1))
-    enc_terms = enc_terms.astype(jnp.bfloat16).reshape(stored, seg_len, enc_width)
-    grad_encoded = lax.psum_scatter(enc_terms, "mp", scatter_dimension=1, tiled=True)
+    parts = lax.axis_size("mp")
+    grad_stored = grad_stored.reshape(stored, parts, seg_len // parts, 2 * head_cols)
+    grad_stored = grad_stored.transpose(1, 0, 2, 3).reshape(parts, -1, 2 * head_cols)
+    grad_encoded = encoded_sum(grad_stored, w_pair)
     return attended, grad_hidden, grad_encoded.reshape(stored, -1)
 
 

time: 414 us -> 236 us (0.57)
  waiting for transfers between devices: 288 us -> 52.2 us
  Pallas kernels: 22 us -> 147 us
  blocking collectives: 48.9 us -> 0 us
  matrix products: 28.7 us -> 13.5 us
  starting transfers between devices: 5.18 us -> 0.04 us
    reduce_scatter x3 -> x0, waiting for transfers between devices: 236 us -> none  [the longest x1 92.3 us: shards(): lax.psum_scatter(grad_terms, 'mp', scatter_dimension=1, tiled=True)]
    pallas_call x0 -> x2, Pallas kernels: none -> 125 us  [the longest x1 87.6 us: exchange(): pl.pallas_call(functools.partial(exchange_kernel, n, owners), in_specs=[v...]
    all_gather x1 -> x0, blocking collectives: 48.9 us -> none  [shards(): ids = lax.all_gather(neighbours.reshape(requests), 'dp', axis=0)]
    dot_general x3 -> x1, matrix products: 12.6 us -> 5.96 us  [dot(): lax.dot_general(a, b, ((contract[:1], contract[1:]), ((), ())), preferred...]
    dot_general x1 -> x0, matrix products: 6.48 us -> none  [shards(): jnp.dot(attn, w_out, preferred_element_type=jnp.float32)]
    all_to_all x1 -> x0, starting transfers between devices: 4.83 us -> none  [shards(): lax.all_to_all(outgoing, 'dp', split_axis=0, concat_axis=0, tiled=True)]
  transfers between devices with their start and end apart: 5 -> 1, of which waited for: 4 -> 1; matrix products, arithmetic and copies ran while one was open for 6% -> 4% of each run, Pallas kernels for 0% -> 0%
where the time goes in v2:
time: 236 us; the launch traced here: 235 us
  Pallas kernels  147 us (62%)
  waiting for transfers between devices  52.2 us (22%)
  between operations  14.2 us (6%)
  matrix products  13.5 us (6%)
  local copies, waits for them, and re-layouts  8.16 us (3%)
    pallas_call x1, Pallas kernels, exchange(): pl.pallas_call(functools.partial(exchange_kernel, n, owners), in_specs=[v...  87.6 us
    all_gather x1, waiting for transfers between devices, shards(): lax.all_gather(kv_own.reshape(stored, seg_len, 2 * head_cols), 'dp', axis...  52.2 us
    pallas_call x1, Pallas kernels, encoded_sum(): pl.pallas_call(functools.partial(encoded_kernel, n), in_specs=[vmem] * 2,...  37.3 us
    pallas_call x1, Pallas kernels, attention(): pl.pallas_call(functools.partial(attention_kernel, per_block), grid_spec=...  17.9 us
    dot_general x1, matrix products, dot(): lax.dot_general(a, b, ((contract[:1], contract[1:]), ((), ())), preferred...  5.96 us
    dot_general x1, matrix products, shards(): jnp.dot(enc_rows, w_pair, preferred_element_type=jnp.float32)  5.22 us
  transfers between devices with their start and end apart: 1, of which 1 were waited for; matrix products, arithmetic and copies ran while one was open for 4% of the time, Pallas kernels for 0%

profile of v2, /device:TPU:0, one launch (start us, length us, event | category | flops | bytes accessed | tf_op | source)
XLA Modules:
  0.0 235.3 jit_solution(11281905988809367318)
XLA Ops:
  7.2 0.0 all-gather.2.cloned.1.call-start
  7.2 1.4 constant_dynamic-update-slice_fusion.1
  8.6 3.6 %reshape.125 = bf16[1024,896]{1,0:T(8,128)(2,1)} reshape(bf16[8,114688]{1,0:T(8,128)(2,1)} %param.9) | data formatting | bytes 3670016 | tf_op jit(solution)/shard_map/reshape | solution.py:297
  12.2 0.1 constant_dynamic-update-slice_fusion.w_pair
  12.3 0.0 copy-start.2
  12.3 5.2 %convolution_convert_fusion = bf16[1024,1024]{0,1:T(8,128)(2,1)} fusion(bf16[1024,896]{1,0:T(8,128)(2,1)} %reshape.125, bf16[896,1024]{1,0:T(8,128)(2,1)S(1)} %constant_dynamic-update-slice_fusion.w_pair), kind=kOutput, calls=%fused_computation | convolution fusion | flops 1880096768 | bytes 5767168 | tf_op jit(solution)/shard_map/dot_general | solution.py:298
  17.6 0.0 all-gather.2.cloned.1.call-update
  17.6 0.1 copy.17
  17.7 0.1 reshape.124.ids
  17.8 0.2 convert_reduce_fusion
  18.0 0.1 select_reduce_fusion
  18.1 0.1 sub.11
  18.2 6.0 %convolution_convert_fusion.1.ga_ref = bf16[512,512]{1,0:T(8,128)(2,1)S(1)} fusion(bf16[512,4096]{1,0:T(8,128)(2,1)} %param.15, bf16[512,4096]{1,0:T(8,128)(2,1)} %w_out.1), kind=kOutput, calls=%fused_computation.1 | convolution fusion | flops 2147745792 | bytes 8912896 | tf_op jit(solution)/shard_map/dot_general | solution.py:16
  24.2 2.3 convolution_convert_fusion.2.q_ref
  26.5 52.2 %all-gather.2.cloned.1.call-done.refs_0_.refs_1_ = bf16[32,128,1024]{2,1,0:T(8,128)(2,1)} async-done(((bf16[8,128,1024]{2,1,0:T(8,128)(2,1)}), bf16[32,128,1024]{2,1,0:T(8,128)(2,1)}) %all-gather.2.cloned.1.call-update) | async-done | bytes 8388624 | tf_op jit(solution)/shard_map/all_gather | solution.py:299
  78.7 17.9 %attention.1 = (bf16[512,512]{1,0:T(8,128)(2,1)S(1)}, bf16[512,512]{1,0:T(8,128)(2,1)S(1)}, bf16[16,128,1024]{2,1,0:T(8,128)(2,1)}) custom-call(s32[16]{0:T(128)S(1)} %reshape.124.ids, s32[16]{0:T(128)S(1)} %multiply_add_fusion.target, bf16[512,512]{1,0:T(8,128)(2,1)S(1)} %convolution_convert_fusion.2.q_ref, ...), custom_call_target="tpu_custom_call" | custom-call | tf_op jit(solution)/shard_map/attention/pallas_call | solution.py:64
  96.7 87.6 %exchange.1 = (bf16[512,512]{1,0:T(8,128)(2,1)S(1)}, bf16[512,512]{1,0:T(8,128)(2,1)S(1)}, bf16[16,128,1024]{2,1,0:T(8,128)(2,1)}, s32[4,8,128]{2,1,0:T(8,128)S(1)}) custom-call(bf16[512,512]{1,0:T(8,128)(2,1)S(1)} %get-tuple-element.10.attn, bf16[512,512]{1,0:T(8,128)(2,1)S(1)} %get-tuple-element.11.gq, bf16[512,4096]{1,0:T(8,128)(2,1)} %w_out.1, ...), custom_call_target="tpu_custom_call" | custom-call | tf_op jit(solution)/shard_map/exchange/pallas_call | solution.py:232
  184.3 0.1 reshape_squeeze.3.ids
  184.4 4.1 %sum_slots.1 = bf16[8,128,1024]{2,1,0:T(8,128)(2,1)S(1)} custom-call(s32[16]{0:T(128)S(1)} %reshape_squeeze.3.ids, bf16[16,128,1024]{2,1,0:T(8,128)(2,1)} %get-tuple-element.16.ret_ref), custom_call_target="tpu_custom_call" | custom-call | tf_op jit(solution)/shard_map/sum_slots/pallas_call | solution.py:98
  188.4 0.3 copy.18
  188.8 37.3 %encoded_sum.1 = bf16[128,896]{1,0:T(8,128)(2,1)S(1)} custom-call(bf16[8,128,1024]{2,1,0:T(8,128)(2,1)S(1)} %bitcast.14, bf16[896,1024]{1,0:T(8,128)(2,1)S(1)} %constant_dynamic-update-slice_fusion.w_pair), custom_call_target="tpu_custom_call" | custom-call | tf_op jit(solution)/shard_map/encoded_sum/pallas_call | solution.py:269
  226.0 0.8 reshape.129
  226.8 0.8 copy.22
  227.6 0.8 copy.23
  (13 shorter events, 0.1 us)
Async XLA Ops:
  7.2 5.0 %copy-start.1 = (bf16[896,512]{1,0:T(8,128)(2,1)S(1)}, bf16[896,512]{1,0:T(8,128)(2,1)}, u32[]{:S(2)}) copy-start(bf16[896,512]{1,0:T(8,128)(2,1)} %param.13) | copy-start | bytes 2752516
  7.2 71.6 %all-gather.2.cloned.1.call-start = ((), (), s32[]{:S(2)}) async-start(), calls=%async_computation | async-start | bytes 10485760 | tf_op jit(solution)/shard_map/all_gather | solution.py:299
  12.3 5.3 %copy-start.2 = (s32[8,2]{0,1:T(2,128)S(1)}, s32[8,2]{0,1:T(2,128)}, u32[]{:S(2)}) copy-start(s32[8,2]{0,1:T(2,128)} %param.10) | copy-start | bytes 196
  18.2 6.0 %copy-start = (bf16[4096,512]{1,0:T(8,128)(2,1)S(1)}, bf16[4096,512]{1,0:T(8,128)(2,1)}, u32[]{:S(2)}) copy-start(bf16[4096,512]{1,0:T(8,128)(2,1)} %w_query.1) | copy-start | bytes 12582916
  18.2 6.0 %copy-start.3 = (bf16[512,4096]{1,0:T(8,128)(2,1)S(1)}, bf16[512,4096]{1,0:T(8,128)(2,1)}, u32[]{:S(2)}) copy-start(bf16[512,4096]{1,0:T(8,128)(2,1)} %param.8) | copy-start | bytes 12582916
Sparse Core Ops, SparseCore 0:
  17.7 60.9 all-gather.1

commit v3 on v1

--- a/solution.py
+++ b/solution.py
@@ -79,40 +79,193 @@
     )(ids, target, queries, grad_attn, *([kv] * per_block))
 
 
-def sum_kernel(count, ids, ret_ref, out_ref, acc):
-    acc[...] = jnp.zeros_like(acc)
-
-    @pl.loop(0, count)
-    def _(i):
-        slot = ids[i]
-
-        @pl.when(slot >= 0)
-        def _():
-            acc[slot] = acc[slot] + ret_ref[i].astype(jnp.float32)
-
-    out_ref[...] = acc[...].astype(jnp.bfloat16)
-
-
-def sum_slots(ids, returned, stored):
-    shape = (stored,) + returned.shape[1:]
+def ring_place(n, index):
+    return jnp.where(index % 2 == 0, index // 2, n - 1 - index // 2)
+
+
+def ring_index(n, place):
+    return jnp.where(place < n // 2, 2 * place, 2 * (n - 1 - place) + 1)
+
+
+def ring_setup(n):
+    forward = 1 - 2 * (lax.axis_index("dp") % 2)
+    place = ring_place(n, lax.axis_index("mp"))
+    ahead = ring_index(n, (place + forward + n) % n)
+    behind = ring_index(n, (place - forward + n) % n)
+
+    def chunk(step):
+        return ring_index(n, (place - forward * (1 + step) + 2 * n) % n)
+
+    return ahead, behind, chunk
+
+
+class Ring:
+    def __init__(self, n, ahead, chunk, part, buf, first, send_sem, recv_sem, out):
+        self.n, self.ahead, self.chunk, self.part = n, ahead, chunk, part
+        self.buf, self.head, self.send_sem, self.recv_sem, self.out = buf, first, send_sem, recv_sem, out
+
+    def copy(self, src, step):
+        return pltpu.make_async_remote_copy(
+            src_ref=src,
+            dst_ref=self.buf.at[step],
+            send_sem=self.send_sem.at[step],
+            recv_sem=self.recv_sem.at[step],
+            device_id={"mp": self.ahead},
+            device_id_type=pl.DeviceIdType.MESH,
+        )
+
+    def first(self):
+        self.head[...] = self.part(self.chunk(0)).astype(jnp.bfloat16)
+        self.copy(self.head, 0).start()
+
+    def middle(self, step):
+        term = self.part(self.chunk(step))
+        held = self.buf.at[step - 1]
+        self.copy(held, step - 1).wait_recv()
+        held[...] = (held[...].astype(jnp.float32) + term).astype(jnp.bfloat16)
+        self.copy(held, step).start()
+
+    def last(self):
+        term = self.part(self.chunk(self.n - 1))
+        self.copy(self.head, self.n - 2).wait_recv()
+        self.out[...] = (self.buf[self.n - 2].astype(jnp.float32) + term).astype(jnp.bfloat16)
+
+    def drain(self):
+        @pl.loop(0, self.n - 1)
+        def _(step):
+            self.copy(self.head, step).wait_send()
+
+
+def exchange_kernel(
+    n, owners, stored, attn, gq, w_out, w_query, w_pair, outgoing, sent_ids,
+    att_out, hid_out, enc_out, returned, returned_ids,
+    att_buf, hid_buf, enc_buf, att_first, hid_first, enc_first,
+    att_send, att_recv, hid_send, hid_recv, enc_send, enc_recv,
+    data_send, data_recv, ids_send, ids_recv, local_sem,
+):
+    me = lax.axis_index("dp")
+    ahead, behind, chunk = ring_setup(n)
+    rows = outgoing.shape[0] // owners
+    width = att_out.shape[1]
+
+    barrier = pltpu.get_barrier_semaphore()
+    for device in [{"mp": ahead}, {"mp": behind}] + [{"dp": (me + d) % owners} for d in range(1, owners)]:
+        pl.semaphore_signal(barrier, inc=1, device_id=device, device_id_type=pl.DeviceIdType.MESH)
+    pl.semaphore_wait(barrier, 1 + owners)
+
+    def block(index):
+        return pl.ds(pl.multiple_of(index * rows, rows), rows)
+
+    copies = []
+    for d in range(1, owners):
+        to = (me + d) % owners
+        for src, dst, send, recv in (
+            (outgoing.at[block(to)], returned.at[block(me)], data_send, data_recv),
+            (sent_ids.at[to], returned_ids.at[me], ids_send, ids_recv),
+        ):
+            copies.append(pltpu.make_async_remote_copy(
+                src_ref=src,
+                dst_ref=dst,
+                send_sem=send.at[d - 1],
+                recv_sem=recv.at[d - 1],
+                device_id={"dp": to},
+                device_id_type=pl.DeviceIdType.MESH,
+            ))
+    local = [
+        pltpu.make_async_copy(outgoing.at[block(me)], returned.at[block(me)], local_sem.at[0]),
+        pltpu.make_async_copy(sent_ids.at[me], returned_ids.at[me], local_sem.at[1]),
+    ]
+    for copy in copies + local:
+        copy.start()
+
+    def at(index):
+        return pl.ds(pl.multiple_of(index * width, width), width)
+
+    tokens = returned.shape[1] // n
+    window = max(tokens, 16)
+    enc_rows = stored * tokens
+
+    def enc_part(c):
+        start = c * tokens
+        base = pl.multiple_of(start // 16 * 16, 16)
+        shape = (enc_rows, rows * window)
+        row = lax.broadcasted_iota(jnp.int32, shape, 0)
+        col = lax.broadcasted_iota(jnp.int32, shape, 1)
+        same_token = col % window == start - base + row % tokens
+        total = None
+        for q in range(owners):
+            slot = returned_ids[q, 0:1, 0:rows * window]
+            hit = jnp.where(same_token & (slot == row // tokens), 1.0, 0.0).astype(jnp.bfloat16)
+            block_rows = returned[q * rows:(q + 1) * rows, pl.ds(base, window), :]
+            term = dot(hit, block_rows.reshape(rows * window, -1), (1, 0))
+            total = term if total is None else total + term
+        return dot(total.astype(jnp.bfloat16), w_pair[...], (1, 1))
+
+    att = Ring(n, ahead, chunk, lambda c: dot(attn[...], w_out[:, at(c)], (1, 0)),
+               att_buf, att_first, att_send, att_recv, att_out)
+    hid = Ring(n, ahead, chunk, lambda c: dot(gq[...], w_query[at(c), :], (1, 1)),
+               hid_buf, hid_first, hid_send, hid_recv, hid_out)
+    enc = Ring(n, ahead, chunk, enc_part, enc_buf, enc_first, enc_send, enc_recv, enc_out)
+
+    alone = n // 2
+    att.first()
+    hid.first()
+
+    @pl.loop(1, alone + 1)
+    def _(step):
+        att.middle(step)
+        hid.middle(step)
+
+    for copy in copies + local:
+        copy.wait()
+    enc.first()
+
+    @pl.loop(alone + 1, n - 1)
+    def _(step):
+        done = 2 * (step - alone - 1)
+        att.middle(step)
+        enc.middle(done + 1)
+        hid.middle(step)
+        enc.middle(done + 2)
+
+    att.last()
+    enc.middle(n - 3)
+    hid.last()
+    enc.middle(n - 2)
+    enc.last()
+    for ring in (att, hid, enc):
+        ring.drain()
+
+
+def exchange(attn, gq, w_out, w_query, w_pair, outgoing, sent_ids, stored):
+    n, owners = lax.axis_size("mp"), lax.axis_size("dp")
+    tok = attn.shape[0]
+    width = w_out.shape[1] // n
+    vmem = pl.BlockSpec(memory_space=pltpu.VMEM)
+    anywhere = pl.BlockSpec(memory_space=pl.ANY)
+    shapes = [(tok, width), (tok, width), (stored * outgoing.shape[1] // n, w_pair.shape[0])]
+    ring = pltpu.SemaphoreType.DMA((n - 1,))
+    peers = pltpu.SemaphoreType.DMA((owners - 1,))
     return pl.pallas_call(
-        functools.partial(sum_kernel, returned.shape[0]),
-        grid_spec=pltpu.PrefetchScalarGridSpec(
-            num_scalar_prefetch=1,
-            grid=(1,),
-            in_specs=[pl.BlockSpec(returned.shape, lambda i, ids: (0, 0, 0))],
-            out_specs=pl.BlockSpec(shape, lambda i, ids: (0, 0, 0)),
-            scratch_shapes=[pltpu.VMEM(shape, jnp.float32)],
+        functools.partial(exchange_kernel, n, owners, stored),
+        in_specs=[vmem] * 5 + [anywhere] * 2,
+        out_specs=[vmem] * 3,
+        out_shape=[jax.ShapeDtypeStruct(shape, jnp.bfloat16) for shape in shapes],
+        scratch_shapes=[pltpu.VMEM(outgoing.shape, outgoing.dtype), pltpu.VMEM(sent_ids.shape, sent_ids.dtype)]
+        + [pltpu.VMEM((n - 1,) + shape, jnp.bfloat16) for shape in shapes]
+        + [pltpu.VMEM(shape, jnp.bfloat16) for shape in shapes]
+        + [ring] * 6
+        + [peers] * 4
+        + [pltpu.SemaphoreType.DMA((2,))],
+        compiler_params=pltpu.CompilerParams(
+            collective_id=1, has_side_effects=True, vmem_limit_bytes=VMEM_BYTES
         ),
-        out_shape=jax.ShapeDtypeStruct(shape, jnp.bfloat16),
-        compiler_params=pltpu.CompilerParams(vmem_limit_bytes=VMEM_BYTES),
-        name="sum_slots",
-    )(ids, returned)
+        name="exchange",
+    )(attn, gq, w_out, w_query, w_pair, outgoing, sent_ids)
 
 
 def shards(hidden, encoded, neighbours, w_query, w_key, w_value, w_out, cotangent):
     owners = lax.axis_size("dp")
-    me = lax.axis_index("dp")
     blocks, per_block = neighbours.shape
     requests = blocks * per_block
     capacity = requests // 4
@@ -127,31 +280,25 @@
     queries = jnp.dot(hidden, w_query, preferred_element_type=jnp.float32).astype(jnp.bfloat16)
     grad_attn = dot(cotangent, w_out, (1, 1)).astype(jnp.bfloat16)
 
-    ids = lax.all_gather(neighbours.reshape(requests), "dp", axis=0)
-    owner_of = ids // stored
-    slot_of = ids % stored
-    same = owner_of[:, :, None] == owner_of[:, None, :]
-    before = jnp.arange(requests)[:, None] > jnp.arange(requests)[None, :]
-    position = jnp.sum((same & before[None]).astype(jnp.int32), axis=2)
-    wanted = (owner_of == me)[:, :, None] & (position[:, :, None] == jnp.arange(capacity)[None, None, :])
-    my_slots = (jnp.sum(jnp.where(wanted, slot_of[:, :, None] + 1, 0), axis=1) - 1).reshape(owners * capacity)
     flat_ids = neighbours.reshape(requests)
     flat_owner = flat_ids // stored
     mine = flat_owner[:, None] == flat_owner[None, :]
+    before = jnp.arange(requests)[:, None] > jnp.arange(requests)[None, :]
     target = flat_owner * capacity + jnp.sum((mine & before).astype(jnp.int32), axis=1)
+    placed = target[:, None] == jnp.arange(owners * capacity)[None, :]
+    sent_ids = jnp.sum(jnp.where(placed, (flat_ids % stored)[:, None] + 1, 0), axis=0) - 1
+    parts = lax.axis_size("mp")
+    window = max(seg_len // parts, 16)
+    sent_ids = jnp.repeat(sent_ids.reshape(owners, 1, capacity), window, axis=2)
+    pad = -capacity * window % 128
+    sent_ids = jnp.pad(jnp.broadcast_to(sent_ids, (owners, 8, capacity * window)), ((0, 0), (0, 0), (0, pad)))
 
     attn, grad_query, outgoing = attention(
         flat_ids, target, queries, grad_attn, kv, blocks, owners * capacity
     )
-    returned = lax.all_to_all(outgoing, "dp", split_axis=0, concat_axis=0, tiled=True)
-    partial_value = jnp.dot(attn, w_out, preferred_element_type=jnp.float32).astype(jnp.bfloat16)
-    attended = lax.psum_scatter(partial_value, "mp", scatter_dimension=1, tiled=True)
-    grad_terms = dot(grad_query, w_query, (1, 1)).astype(jnp.bfloat16)
-    grad_hidden = lax.psum_scatter(grad_terms, "mp", scatter_dimension=1, tiled=True)
-    grad_stored = sum_slots(my_slots, returned, stored)
-    enc_terms = dot(grad_stored.reshape(stored * seg_len, 2 * head_cols), w_pair, (1, 1))
-    enc_terms = enc_terms.astype(jnp.bfloat16).reshape(stored, seg_len, enc_width)
-    grad_encoded = lax.psum_scatter(enc_terms, "mp", scatter_dimension=1, tiled=True)
+    attended, grad_hidden, grad_encoded = exchange(
+        attn, grad_query, w_out, w_query, w_pair, outgoing, sent_ids, stored
+    )
     return attended, grad_hidden, grad_encoded.reshape(stored, -1)
 
 

time: 414 us -> 217 us (0.52)
  waiting for transfers between devices: 288 us -> 52.1 us
  Pallas kernels: 22 us -> 129 us
  blocking collectives: 48.9 us -> 0 us
  matrix products: 28.7 us -> 13.5 us
  starting transfers between devices: 5.18 us -> 0.04 us
    reduce_scatter x3 -> x0, waiting for transfers between devices: 236 us -> none  [the longest x1 92.3 us: shards(): lax.psum_scatter(grad_terms, 'mp', scatter_dimension=1, tiled=True)]
    pallas_call x1, Pallas kernels: 4.08 us -> 111 us  [exchange(): pl.pallas_call(functools.partial(exchange_kernel, n, owners, stored), in_...]
    all_gather x1 -> x0, blocking collectives: 48.9 us -> none  [shards(): ids = lax.all_gather(neighbours.reshape(requests), 'dp', axis=0)]
    dot_general x3 -> x1, matrix products: 12.6 us -> 5.96 us  [dot(): lax.dot_general(a, b, ((contract[:1], contract[1:]), ((), ())), preferred...]
    dot_general x1 -> x0, matrix products: 6.48 us -> none  [shards(): jnp.dot(attn, w_out, preferred_element_type=jnp.float32)]
    all_to_all x1 -> x0, starting transfers between devices: 4.83 us -> none  [shards(): lax.all_to_all(outgoing, 'dp', split_axis=0, concat_axis=0, tiled=True)]
  transfers between devices with their start and end apart: 5 -> 1, of which waited for: 4 -> 1; matrix products, arithmetic and copies ran while one was open for 6% -> 4% of each run, Pallas kernels for 0% -> 0%
where the time goes in v3:
time: 217 us
  Pallas kernels  129 us (59%)
  waiting for transfers between devices  52.1 us (24%)
  between operations  14.1 us (6%)
  matrix products  13.5 us (6%)
  local copies, waits for them, and re-layouts  7.91 us (4%)
    pallas_call x1, Pallas kernels, exchange(): pl.pallas_call(functools.partial(exchange_kernel, n, owners, stored), in_...  111 us
    all_gather x1, waiting for transfers between devices, shards(): lax.all_gather(kv_own.reshape(stored, seg_len, 2 * head_cols), 'dp', axis...  52.1 us
    pallas_call x1, Pallas kernels, attention(): pl.pallas_call(functools.partial(attention_kernel, per_block), grid_spec=...  18.1 us
    dot_general x1, matrix products, dot(): lax.dot_general(a, b, ((contract[:1], contract[1:]), ((), ())), preferred...  5.96 us
    dot_general x1, matrix products, shards(): jnp.dot(enc_rows, w_pair, preferred_element_type=jnp.float32)  5.2 us
  transfers between devices with their start and end apart: 1, of which 1 were waited for; matrix products, arithmetic and copies ran while one was open for 4% of the time, Pallas kernels for 0%

profile of v3, /device:TPU:0, one launch (start us, length us, event | category | flops | bytes accessed | tf_op | source)
XLA Modules:
  0.0 217.2 jit_solution(17625054270798005747)
XLA Ops:
  7.2 0.0 all-gather.2.cloned.1.call-start
  7.2 1.4 constant_dynamic-update-slice_fusion.1
  8.6 3.6 %reshape.121 = bf16[1024,896]{1,0:T(8,128)(2,1)} reshape(bf16[8,114688]{1,0:T(8,128)(2,1)} %param.9) | data formatting | bytes 3670016 | tf_op jit(solution)/shard_map/reshape | solution.py:277
  12.2 0.1 constant_dynamic-update-slice_fusion.w_pair
  12.3 0.0 copy-start.2
  12.3 5.2 %convolution_convert_fusion = bf16[1024,1024]{0,1:T(8,128)(2,1)} fusion(bf16[1024,896]{1,0:T(8,128)(2,1)} %reshape.121, bf16[896,1024]{1,0:T(8,128)(2,1)S(1)} %constant_dynamic-update-slice_fusion.w_pair), kind=kOutput, calls=%fused_computation | convolution fusion | flops 1880096768 | bytes 5767168 | tf_op jit(solution)/shard_map/dot_general | solution.py:278
  17.5 0.0 all-gather.2.cloned.1.call-update
  17.6 0.1 copy.14
  17.7 0.1 reshape.120.ids
  17.8 0.2 convert_reduce_fusion
  17.9 0.1 select_reduce_fusion
  18.0 0.1 sub.11
  18.1 0.1 broadcast_in_dim.31
  18.2 0.1 broadcast_in_dim.32
  18.3 0.0 copy-start
  18.3 0.0 copy-start.3
  18.3 6.0 %convolution_convert_fusion.1.ga_ref = bf16[512,512]{1,0:T(8,128)(2,1)S(1)} fusion(bf16[512,4096]{1,0:T(8,128)(2,1)} %param.15, bf16[512,4096]{1,0:T(8,128)(2,1)} %w_out.1), kind=kOutput, calls=%fused_computation.1 | convolution fusion | flops 2147745792 | bytes 8912896 | tf_op jit(solution)/shard_map/dot_general | solution.py:16
  24.3 2.3 %convolution_convert_fusion.2.q_ref = bf16[512,512]{1,0:T(8,128)(2,1)S(1)} fusion(bf16[512,4096]{1,0:T(8,128)(2,1)S(1)} %copy-done.3, bf16[4096,512]{1,0:T(8,128)(2,1)S(1)} %copy-done), kind=kOutput, calls=%fused_computation.2 | convolution fusion | flops 2147745792 | bytes 8912896 | tf_op jit(solution)/shard_map/dot_general | solution.py:280
  26.6 52.1 %all-gather.2.cloned.1.call-done.refs_0_.refs_1_ = bf16[32,128,1024]{2,1,0:T(8,128)(2,1)} async-done(((bf16[8,128,1024]{2,1,0:T(8,128)(2,1)}), bf16[32,128,1024]{2,1,0:T(8,128)(2,1)}) %all-gather.2.cloned.1.call-update) | async-done | bytes 8388624 | tf_op jit(solution)/shard_map/all_gather | solution.py:279
  78.7 18.1 %attention.1 = (bf16[512,512]{1,0:T(8,128)(2,1)S(1)}, bf16[512,512]{1,0:T(8,128)(2,1)S(1)}, bf16[16,128,1024]{2,1,0:T(8,128)(2,1)}) custom-call(s32[16]{0:T(128)S(1)} %reshape.120.ids, s32[16]{0:T(128)S(1)} %multiply_add_fusion.target, bf16[512,512]{1,0:T(8,128)(2,1)S(1)} %convolution_convert_fusion.2.q_ref, ...), custom_call_target="tpu_custom_call" | custom-call | tf_op jit(solution)/shard_map/attention/pallas_call | solution.py:64
  96.8 111.1 %exchange.1 = (bf16[512,512]{1,0:T(8,128)(2,1)S(1)}, bf16[512,512]{1,0:T(8,128)(2,1)S(1)}, bf16[128,896]{1,0:T(8,128)(2,1)S(1)}) custom-call(bf16[512,512]{1,0:T(8,128)(2,1)S(1)} %get-tuple-element.9.attn, bf16[512,512]{1,0:T(8,128)(2,1)S(1)} %get-tuple-element.10.gq, bf16[512,4096]{1,0:T(8,128)(2,1)} %w_out.1, bf16[4096,512]{1,0:T(8,128)(2,1)} %w_query.1, ...), custom_call_target="tpu_custom_call" | custom-call | tf_op jit(solution)/shard_map/exchange/pallas_call | solution.py:249
  207.9 0.8 reshape.123
  208.7 0.8 copy.18
  209.5 0.8 copy.19
  (10 shorter events, 0.1 us)
Async XLA Ops:
  7.2 5.0 %copy-start.1 = (bf16[896,512]{1,0:T(8,128)(2,1)S(1)}, bf16[896,512]{1,0:T(8,128)(2,1)}, u32[]{:S(2)}) copy-start(bf16[896,512]{1,0:T(8,128)(2,1)} %param.13) | copy-start | bytes 2752516
  7.2 71.5 %all-gather.2.cloned.1.call-start = ((), (), s32[]{:S(2)}) async-start(), calls=%async_computation | async-start | bytes 10485760 | tf_op jit(solution)/shard_map/all_gather | solution.py:279
  12.3 5.2 %copy-start.2 = (s32[8,2]{0,1:T(2,128)S(1)}, s32[8,2]{0,1:T(2,128)}, u32[]{:S(2)}) copy-start(s32[8,2]{0,1:T(2,128)} %param.10) | copy-start | bytes 196
  18.3 6.0 %copy-start = (bf16[4096,512]{1,0:T(8,128)(2,1)S(1)}, bf16[4096,512]{1,0:T(8,128)(2,1)}, u32[]{:S(2)}) copy-start(bf16[4096,512]{1,0:T(8,128)(2,1)} %w_query.1) | copy-start | bytes 12582916
  18.3 6.0 %copy-start.3 = (bf16[512,4096]{1,0:T(8,128)(2,1)S(1)}, bf16[512,4096]{1,0:T(8,128)(2,1)}, u32[]{:S(2)}) copy-start(bf16[512,4096]{1,0:T(8,128)(2,1)} %param.8) | copy-start | bytes 12582916
Sparse Core Ops, SparseCore 0:
  17.7 60.9 all-gather.1

commit v4 on v3

--- a/solution.py
+++ b/solution.py
@@ -264,6 +264,162 @@
     )(attn, gq, w_out, w_query, w_pair, outgoing, sent_ids)
 
 
+def fetch_kernel(
+    nx, rows, hidden, w_query, cotangent, w_out, w_pair, queries, grad_attn, kv,
+    held, hid_v, wq_v, cot_v, wo_v,
+    load_sem, x_send, x_recv, y_send, y_recv, own_send, own_recv,
+    cx_send, cx_recv, cy_send, cy_recv,
+):
+    me, mp = lax.axis_index("dp"), lax.axis_index("mp")
+    stored, seg, width = rows.shape
+    half = stored // 2
+    x, core, side = me // 2, me % 2, mp % 2
+    twin = {"dp": x * 2 + 1 - core}
+    pair = {"mp": mp + 1 - 2 * side}
+    away = [{"dp": (x + d) % nx * 2 + core} for d in range(1, nx)]
+    source = [(x - d + nx) % nx * 2 for d in range(1, nx)]
+
+    barrier = pltpu.get_barrier_semaphore()
+    for device in away + [twin, pair]:
+        pl.semaphore_signal(barrier, inc=1, device_id=device, device_id_type=pl.DeviceIdType.MESH)
+    pl.semaphore_wait(barrier, nx + 1)
+
+    def send(src, place, sems, index, device):
+        return pltpu.make_async_remote_copy(
+            src_ref=src,
+            dst_ref=held.at[place],
+            send_sem=sems[0].at[index],
+            recv_sem=sems[1].at[index],
+            device_id=device,
+            device_id_type=pl.DeviceIdType.MESH,
+        )
+
+    def relay(place, sems, index, device):
+        return send(held.at[place], place, sems, index, device)
+
+    steps = [(d, r) for r in range(half) for d in range(nx - 1)]
+    mine, other = side * half, (1 - side) * half
+    x_copies = [
+        send(rows.at[mine + r], me * stored + mine + r, (x_send, x_recv), d * half + r, away[d])
+        for d, r in steps
+    ]
+    own = send(rows, pl.ds(me * stored, stored), (own_send, own_recv), 0, twin)
+    for copy in x_copies + [own]:
+        copy.start()
+    loads = [
+        pltpu.make_async_copy(src, dst, load_sem.at[i])
+        for i, (src, dst) in enumerate(((hidden, hid_v), (w_query, wq_v), (cotangent, cot_v), (w_out, wo_v)))
+    ]
+    for load in loads:
+        load.start()
+
+    def project(src, first, place):
+        block = src[pl.ds(first, half)].reshape(half * seg, width)
+        out = dot(block, w_pair[...], (1, 0)).astype(jnp.bfloat16)
+        kv[pl.ds(place, half)] = out.reshape(half, seg, -1)
+
+    y_copies, cx_copies, cy_copies = [], [], []
+
+    def pass_on(at):
+        d, r = steps[at]
+        place = (source[d] + core) * stored + mine + r
+        x_copies[at].wait_recv()
+        y_copies.append(relay(place, (y_send, y_recv), d * half + r, pair))
+        cx_copies.append(relay(place, (cx_send, cx_recv), d * half + r, twin))
+        y_copies[-1].start()
+        cx_copies[-1].start()
+
+    def finish(at):
+        d, r = steps[at]
+        place = (source[d] + core) * stored + other + r
+        y_copies[at].wait_recv()
+        cy_copies.append(relay(place, (cy_send, cy_recv), d * half + r, twin))
+        cy_copies[-1].start()
+
+    @pl.loop(0, 2)
+    def _(i):
+        project(rows, i * half, me * stored + i * half)
+
+    quarter = len(steps) // 4
+    pass_next = 0
+    for _ in range(quarter):
+        pass_on(pass_next)
+        pass_next += 1
+    loads[0].wait()
+    loads[1].wait()
+    queries[...] = dot(hid_v[...], wq_v[...], (1, 0)).astype(jnp.bfloat16)
+    for _ in range(quarter):
+        pass_on(pass_next)
+        pass_next += 1
+    loads[2].wait()
+    loads[3].wait()
+    grad_attn[...] = dot(cot_v[...], wo_v[...], (1, 1)).astype(jnp.bfloat16)
+    for _ in range(quarter):
+        pass_on(pass_next)
+        pass_next += 1
+    own.wait_recv()
+
+    @pl.loop(0, 2)
+    def _(i):
+        first = (x * 2 + 1 - core) * stored + i * half
+        project(held, first, first)
+
+    while pass_next < len(steps):
+        pass_on(pass_next)
+        pass_next += 1
+    early = max(len(steps) - nx + 1, 0)
+    for at in range(early):
+        finish(at)
+    for copy in cx_copies:
+        copy.wait_recv()
+
+    def project_all(first):
+        for d in range(nx - 1):
+            @pl.loop(0, 2)
+            def _(i):
+                place = (source[d] + i) * stored + first
+                project(held, place, place)
+
+    project_all(mine)
+    for at in range(early, len(steps)):
+        finish(at)
+    for copy in cy_copies:
+        copy.wait_recv()
+    project_all(other)
+    for copy in x_copies + [own] + y_copies + cx_copies + cy_copies:
+        copy.wait_send()
+
+
+def fetch(rows, hidden, w_query, cotangent, w_out, w_pair):
+    owners = lax.axis_size("dp")
+    nx = owners // 2
+    stored, seg, _ = rows.shape
+    vmem = pl.BlockSpec(memory_space=pltpu.VMEM)
+    anywhere = pl.BlockSpec(memory_space=pl.ANY)
+    tok, cols = hidden.shape[0], w_query.shape[1]
+    pieces = pltpu.SemaphoreType.DMA(((nx - 1) * stored // 2,))
+    return pl.pallas_call(
+        functools.partial(fetch_kernel, nx),
+        in_specs=[vmem] + [anywhere] * 4 + [vmem],
+        out_specs=[vmem] * 3,
+        out_shape=[
+            jax.ShapeDtypeStruct((tok, cols), jnp.bfloat16),
+            jax.ShapeDtypeStruct((tok, cols), jnp.bfloat16),
+            jax.ShapeDtypeStruct((owners * stored, seg, w_pair.shape[1]), jnp.bfloat16),
+        ],
+        scratch_shapes=[pltpu.VMEM((owners * stored,) + rows.shape[1:], jnp.bfloat16)]
+        + [pltpu.VMEM(a.shape, a.dtype) for a in (hidden, w_query, cotangent, w_out)]
+        + [pltpu.SemaphoreType.DMA((4,))]
+        + [pieces] * 4
+        + [pltpu.SemaphoreType.DMA((1,))] * 2
+        + [pieces] * 4,
+        compiler_params=pltpu.CompilerParams(
+            collective_id=3, has_side_effects=True, vmem_limit_bytes=VMEM_BYTES
+        ),
+        name="fetch",
+    )(rows, hidden, w_query, cotangent, w_out, w_pair)
+
+
 def shards(hidden, encoded, neighbours, w_query, w_key, w_value, w_out, cotangent):
     owners = lax.axis_size("dp")
     blocks, per_block = neighbours.shape
@@ -274,12 +430,9 @@
     seg_len = encoded.shape[1] // enc_width
 
     w_pair = jnp.concatenate([w_key, w_value], axis=1)
-    enc_rows = encoded.reshape(stored * seg_len, enc_width)
-    kv_own = jnp.dot(enc_rows, w_pair, preferred_element_type=jnp.float32).astype(jnp.bfloat16)
-    kv = lax.all_gather(kv_own.reshape(stored, seg_len, 2 * head_cols), "dp", axis=0, tiled=True)
-    queries = jnp.dot(hidden, w_query, preferred_element_type=jnp.float32).astype(jnp.bfloat16)
-    grad_attn = dot(cotangent, w_out, (1, 1)).astype(jnp.bfloat16)
-
+    queries, grad_attn, kv = fetch(
+        encoded.reshape(stored, seg_len, enc_width), hidden, w_query, cotangent, w_out, w_pair
+    )
     flat_ids = neighbours.reshape(requests)
     flat_owner = flat_ids // stored
     mine = flat_owner[:, None] == flat_owner[None, :]

time: 217 us -> 176 us (0.81)
  waiting for transfers between devices: 52.1 us -> 0 us
  Pallas kernels: 129 us -> 166 us
  matrix products: 13.5 us -> 0 us
  between operations: 14.1 us -> 0.71 us
    all_gather x1 -> x0, waiting for transfers between devices: 52.1 us -> none  [shards(): lax.all_gather(kv_own.reshape(stored, seg_len, 2 * head_cols), 'dp', axis...]
    pallas_call x0 -> x1, Pallas kernels: none -> 36.9 us  [fetch(): pl.pallas_call(functools.partial(fetch_kernel, nx), in_specs=[vmem] + [an...]
    dot_general x3 -> x0, matrix products: 13.5 us -> none  [the longest x1 5.96 us: dot(): lax.dot_general(a, b, ((contract[:1], contract[1:]), ((), ())), preferred...]
    unnamed x12 -> x13, local copies, waits for them, and re-layouts: 3.06 us -> 6.89 us
    reshape x1 -> x0, local copies, waits for them, and re-layouts: 3.59 us -> none  [shards(): enc_rows = encoded.reshape(stored * seg_len, enc_width)]
  transfers between devices with their start and end apart: 1 -> 0, of which waited for: 1 -> 0; matrix products, arithmetic and copies ran while one was open for 4% -> 0% of each run, Pallas kernels for 0% -> 0%
where the time goes in v4:
time: 176 us
  Pallas kernels  166 us (94%)
  local copies, waits for them, and re-layouts  9.09 us (5%)
    pallas_call x1, Pallas kernels, exchange(): pl.pallas_call(functools.partial(exchange_kernel, n, owners, stored), in_...  111 us
    pallas_call x1, Pallas kernels, fetch(): pl.pallas_call(functools.partial(fetch_kernel, nx), in_specs=[vmem] + [an...  36.9 us
    pallas_call x1, Pallas kernels, attention(): pl.pallas_call(functools.partial(attention_kernel, per_block), grid_spec=...  17.9 us
    unnamed x13, local copies, waits for them, and re-layouts  6.89 us

profile of v4, /device:TPU:0, one launch (start us, length us, event | category | flops | bytes accessed | tf_op | source)
XLA Modules:
  0.0 175.9 jit_solution(14518838979755634614)
XLA Ops:
  0.6 0.0 copy-start.3
  0.6 0.8 copy.13
  1.5 0.1 reshape.117.ids
  1.6 0.2 convert_reduce_fusion
  1.8 0.0 copy-start.2
  1.8 1.4 constant_dynamic-update-slice_fusion.1
  3.2 0.0 copy-done.3
  3.2 0.1 constant_dynamic-update-slice_fusion.w_pair
  3.4 0.2 copy-done.2
  3.6 0.3 copy.16
  3.9 36.9 %fetch.1 = (bf16[512,512]{1,0:T(8,128)(2,1)S(1)}, bf16[512,512]{1,0:T(8,128)(2,1)S(1)}, bf16[32,128,1024]{2,1,0:T(8,128)(2,1)}) custom-call(bf16[8,128,896]{2,1,0:T(8,128)(2,1)S(1)} %bitcast.4, bf16[512,4096]{1,0:T(8,128)(2,1)} %hidden.1, bf16[4096,512]{1,0:T(8,128)(2,1)} %w_query.3, bf16[512,4096]{1,0:T(8,128)(2,1)} %cotangent.1, bf16[512,4096]{1,0:T(8,128)(2,1)} %w_out.3, ...), custom_call_target="tpu_custom_call" | custom-call | tf_op jit(solution)/shard_map/fetch/pallas_call | solution.py:401
  40.7 17.9 %attention.1 = (bf16[512,512]{1,0:T(8,128)(2,1)S(1)}, bf16[512,512]{1,0:T(8,128)(2,1)S(1)}, bf16[16,128,1024]{2,1,0:T(8,128)(2,1)}) custom-call(s32[16]{0:T(128)S(1)} %reshape.117.ids, s32[16]{0:T(128)S(1)} %multiply_add_fusion.target, bf16[512,512]{1,0:T(8,128)(2,1)S(1)} %get-tuple-element.12.q_ref, bf16[512,512]{1,0:T(8,128)(2,1)S(1)} %get-tuple-element.13.ga_ref, ...), custom_call_target="tpu_custom_call" | custom-call | tf_op jit(solution)/shard_map/attention/pallas_call | solution.py:64
  58.7 0.1 select_reduce_fusion
  58.7 0.1 sub.11
  58.8 0.1 broadcast_in_dim.31
  58.9 0.1 broadcast_in_dim.32
  59.0 111.0 %exchange.1 = (bf16[512,512]{1,0:T(8,128)(2,1)S(1)}, bf16[512,512]{1,0:T(8,128)(2,1)S(1)}, bf16[128,896]{1,0:T(8,128)(2,1)S(1)}) custom-call(bf16[512,512]{1,0:T(8,128)(2,1)S(1)} %get-tuple-element.15.attn, bf16[512,512]{1,0:T(8,128)(2,1)S(1)} %get-tuple-element.16.gq, bf16[512,4096]{1,0:T(8,128)(2,1)} %w_out.3, bf16[4096,512]{1,0:T(8,128)(2,1)} %w_query.3, ...), custom_call_target="tpu_custom_call" | custom-call | tf_op jit(solution)/shard_map/exchange/pallas_call | solution.py:249
  170.0 0.0 copy-start
  170.0 0.8 copy-done
  170.8 0.0 copy-start.1
  170.8 0.7 copy-done.1
  171.5 1.7 reshape.119
  173.2 1.9 %copy.20 = bf16[512,512]{1,0:T(8,128)(2,1)} copy(bf16[512,512]{1,0:T(8,128)(2,1)} %copy-done) | data formatting | bytes 1048576
  175.1 0.8 copy.21
  (5 shorter events, 0.0 us)
Async XLA Ops:
  0.6 2.6 %copy-start.3 = (bf16[896,512]{1,0:T(8,128)(2,1)S(1)}, bf16[896,512]{1,0:T(8,128)(2,1)}, u32[]{:S(2)}) copy-start(bf16[896,512]{1,0:T(8,128)(2,1)} %param.13) | copy-start | bytes 2752516
  1.8 1.8 %copy-start.2 = (bf16[8,114688]{1,0:T(8,128)(2,1)S(1)}, bf16[8,114688]{1,0:T(8,128)(2,1)}, u32[]{:S(2)}) copy-start(bf16[8,114688]{1,0:T(8,128)(2,1)} %param.9) | copy-start | bytes 5505028
  170.0 0.8 copy-start
  170.8 0.7 copy-start.1

commit v5 on v4

--- a/solution.py
+++ b/solution.py
@@ -29,22 +29,24 @@
         def _():
             out_ref[...] = jnp.zeros_like(out_ref)
 
-    for h in range(cols // DH):
-        at = h * DH
-        q = q_ref[:, at:at + DH]
-        ga = ga_ref[:, at:at + DH]
-        k = jnp.concatenate([r[0, :, at:at + DH] for r in kv_refs], axis=0)
-        v = jnp.concatenate([r[0, :, cols + at:cols + at + DH] for r in kv_refs], axis=0)
-        scores = dot(q, k, (1, 1)) * inv_root
-        grad_prob = dot(ga, v, (1, 1))
-        terms = jnp.exp(scores - jnp.max(scores, axis=-1, keepdims=True))
-        prob = terms / jnp.sum(terms, axis=-1, keepdims=True)
-        half = prob.astype(jnp.bfloat16)
-        attn_ref[:, at:at + DH] = dot(half, v, (1, 0)).astype(jnp.bfloat16)
-        grad_v = dot(half, ga, (0, 0)).astype(jnp.bfloat16)
-        gs = (prob * (grad_prob - jnp.sum(prob * grad_prob, axis=-1, keepdims=True))).astype(jnp.bfloat16)
-        gq_ref[:, at:at + DH] = (dot(gs, k, (1, 0)) * inv_root).astype(jnp.bfloat16)
-        grad_k = (dot(gs, q, (0, 0)) * inv_root).astype(jnp.bfloat16)
+    heads = range(0, cols, DH)
+    q = [q_ref[:, at:at + DH] for at in heads]
+    ga = [ga_ref[:, at:at + DH] for at in heads]
+    k = [jnp.concatenate([r[0, :, at:at + DH] for r in kv_refs], axis=0) for at in heads]
+    v = [jnp.concatenate([r[0, :, cols + at:cols + at + DH] for r in kv_refs], axis=0) for at in heads]
+    scores = [dot(a, b, (1, 1)) * inv_root for a, b in zip(q, k)]
+    grad_prob = [dot(a, b, (1, 1)) for a, b in zip(ga, v)]
+    terms = [jnp.exp(a - jnp.max(a, axis=-1, keepdims=True)) for a in scores]
+    prob = [a / jnp.sum(a, axis=-1, keepdims=True) for a in terms]
+    half = [a.astype(jnp.bfloat16) for a in prob]
+    inner = [jnp.sum(a * b, axis=-1, keepdims=True) for a, b in zip(prob, grad_prob)]
+    gs = [(a * (b - c)).astype(jnp.bfloat16) for a, b, c in zip(prob, grad_prob, inner)]
+    for h, at in enumerate(heads):
+        attn_ref[:, at:at + DH] = dot(half[h], v[h], (1, 0)).astype(jnp.bfloat16)
+        gq_ref[:, at:at + DH] = (dot(gs[h], k[h], (1, 0)) * inv_root).astype(jnp.bfloat16)
+    for h, at in enumerate(heads):
+        grad_v = dot(half[h], ga[h], (0, 0)).astype(jnp.bfloat16)
+        grad_k = (dot(gs[h], q[h], (0, 0)) * inv_root).astype(jnp.bfloat16)
         for j in range(per_block):
             slot = target[step * per_block + j]
             out_ref[slot, :, at:at + DH] = grad_k[j * seg:(j + 1) * seg]
@@ -137,8 +139,8 @@
 
 
 def exchange_kernel(
-    n, owners, stored, attn, gq, w_out, w_query, w_pair, outgoing, sent_ids,
-    att_out, hid_out, enc_out, returned, returned_ids,
+    n, owners, stored, attn, gq, w_out_hbm, w_query_hbm, w_pair, outgoing, sent_ids,
+    att_out, hid_out, enc_out, w_out, w_query, load_sem, returned, returned_ids,
     att_buf, hid_buf, enc_buf, att_first, hid_first, enc_first,
     att_send, att_recv, hid_send, hid_recv, enc_send, enc_recv,
     data_send, data_recv, ids_send, ids_recv, local_sem,
@@ -152,6 +154,12 @@
     for device in [{"mp": ahead}, {"mp": behind}] + [{"dp": (me + d) % owners} for d in range(1, owners)]:
         pl.semaphore_signal(barrier, inc=1, device_id=device, device_id_type=pl.DeviceIdType.MESH)
     pl.semaphore_wait(barrier, 1 + owners)
+    loads = [
+        pltpu.make_async_copy(w_out_hbm, w_out, load_sem.at[0]),
+        pltpu.make_async_copy(w_query_hbm, w_query, load_sem.at[1]),
+    ]
+    for load in loads:
+        load.start()
 
     def block(index):
         return pl.ds(pl.multiple_of(index * rows, rows), rows)
@@ -207,8 +215,10 @@
                hid_buf, hid_first, hid_send, hid_recv, hid_out)
     enc = Ring(n, ahead, chunk, enc_part, enc_buf, enc_first, enc_send, enc_recv, enc_out)
 
-    alone = n // 2
+    alone = n // 2 - 1
+    loads[0].wait()
     att.first()
+    loads[1].wait()
     hid.first()
 
     @pl.loop(1, alone + 1)
@@ -216,22 +226,24 @@
         att.middle(step)
         hid.middle(step)
 
+    att.middle(alone + 1)
     for copy in copies + local:
         copy.wait()
     enc.first()
-
-    @pl.loop(alone + 1, n - 1)
+    hid.middle(alone + 1)
+    enc.middle(1)
+
+    @pl.loop(alone + 2, n - 1)
     def _(step):
         done = 2 * (step - alone - 1)
         att.middle(step)
+        enc.middle(done)
+        hid.middle(step)
         enc.middle(done + 1)
-        hid.middle(step)
-        enc.middle(done + 2)
 
     att.last()
-    enc.middle(n - 3)
+    enc.middle(n - 2)
     hid.last()
-    enc.middle(n - 2)
     enc.last()
     for ring in (att, hid, enc):
         ring.drain()
@@ -248,10 +260,12 @@
     peers = pltpu.SemaphoreType.DMA((owners - 1,))
     return pl.pallas_call(
         functools.partial(exchange_kernel, n, owners, stored),
-        in_specs=[vmem] * 5 + [anywhere] * 2,
+        in_specs=[vmem] * 2 + [anywhere] * 2 + [vmem] + [anywhere] * 2,
         out_specs=[vmem] * 3,
         out_shape=[jax.ShapeDtypeStruct(shape, jnp.bfloat16) for shape in shapes],
-        scratch_shapes=[pltpu.VMEM(outgoing.shape, outgoing.dtype), pltpu.VMEM(sent_ids.shape, sent_ids.dtype)]
+        scratch_shapes=[pltpu.VMEM(w.shape, w.dtype) for w in (w_out, w_query)]
+        + [pltpu.SemaphoreType.DMA((2,))]
+        + [pltpu.VMEM(outgoing.shape, outgoing.dtype), pltpu.VMEM(sent_ids.shape, sent_ids.dtype)]
         + [pltpu.VMEM((n - 1,) + shape, jnp.bfloat16) for shape in shapes]
         + [pltpu.VMEM(shape, jnp.bfloat16) for shape in shapes]
         + [ring] * 6

time: 176 us -> 165 us (0.938)
  Pallas kernels: 166 us -> 154 us
    pallas_call x1, Pallas kernels: 17.9 us -> 10.9 us  [attention(): pl.pallas_call(functools.partial(attention_kernel, per_block), grid_spec=...]
    pallas_call x1, Pallas kernels: 111 us -> 107 us  [exchange(): pl.pallas_call(functools.partial(exchange_kernel, n, owners, stored), in_...]
where the time goes in v5:
time: 165 us; the launch traced here: 164 us
  Pallas kernels  154 us (93%)
  local copies, waits for them, and re-layouts  9.09 us (6%)
    pallas_call x1, Pallas kernels, exchange(): pl.pallas_call(functools.partial(exchange_kernel, n, owners, stored), in_...  107 us
    pallas_call x1, Pallas kernels, fetch(): pl.pallas_call(functools.partial(fetch_kernel, nx), in_specs=[vmem] + [an...  36.9 us
    pallas_call x1, Pallas kernels, attention(): pl.pallas_call(functools.partial(attention_kernel, per_block), grid_spec=...  10.9 us
    unnamed x13, local copies, waits for them, and re-layouts  6.89 us

profile of v5, /device:TPU:0, one launch (start us, length us, event | category | flops | bytes accessed | tf_op | source)
XLA Modules:
  0.0 164.4 jit_solution(5367324730135141363)
XLA Ops:
  0.6 0.0 copy-start.3
  0.6 0.8 copy.13
  1.5 0.1 reshape.117.ids
  1.6 0.2 convert_reduce_fusion
  1.8 0.0 copy-start.2
  1.8 1.4 constant_dynamic-update-slice_fusion.1
  3.2 0.0 copy-done.3
  3.2 0.1 constant_dynamic-update-slice_fusion.w_pair
  3.4 0.2 copy-done.2
  3.6 0.3 copy.16
  3.9 36.9 %fetch.1 = (bf16[512,512]{1,0:T(8,128)(2,1)S(1)}, bf16[512,512]{1,0:T(8,128)(2,1)S(1)}, bf16[32,128,1024]{2,1,0:T(8,128)(2,1)}) custom-call(bf16[8,128,896]{2,1,0:T(8,128)(2,1)S(1)} %bitcast.4, bf16[512,4096]{1,0:T(8,128)(2,1)} %hidden.1, bf16[4096,512]{1,0:T(8,128)(2,1)} %w_query_hbm.1, bf16[512,4096]{1,0:T(8,128)(2,1)} %cotangent.1, ...), custom_call_target="tpu_custom_call" | custom-call | tf_op jit(solution)/shard_map/fetch/pallas_call | solution.py:415
  40.7 10.9 %attention.1 = (bf16[512,512]{1,0:T(8,128)(2,1)S(1)}, bf16[512,512]{1,0:T(8,128)(2,1)S(1)}, bf16[16,128,1024]{2,1,0:T(8,128)(2,1)}) custom-call(s32[16]{0:T(128)S(1)} %reshape.117.ids, s32[16]{0:T(128)S(1)} %multiply_add_fusion.target, bf16[512,512]{1,0:T(8,128)(2,1)S(1)} %get-tuple-element.12.q_ref, bf16[512,512]{1,0:T(8,128)(2,1)S(1)} %get-tuple-element.13.ga_ref, ...), custom_call_target="tpu_custom_call" | custom-call | tf_op jit(solution)/shard_map/attention/pallas_call | solution.py:66
  51.6 0.1 select_reduce_fusion
  51.7 0.1 sub.11
  51.8 0.1 broadcast_in_dim.31
  51.8 0.1 broadcast_in_dim.32
  51.9 106.6 %exchange.1 = (bf16[512,512]{1,0:T(8,128)(2,1)S(1)}, bf16[512,512]{1,0:T(8,128)(2,1)S(1)}, bf16[128,896]{1,0:T(8,128)(2,1)S(1)}) custom-call(bf16[512,512]{1,0:T(8,128)(2,1)S(1)} %get-tuple-element.15.attn, bf16[512,512]{1,0:T(8,128)(2,1)S(1)} %get-tuple-element.16.gq, bf16[512,4096]{1,0:T(8,128)(2,1)} %w_out_hbm.1, bf16[4096,512]{1,0:T(8,128)(2,1)} %w_query_hbm.1, ...), custom_call_target="tpu_custom_call" | custom-call | tf_op jit(solution)/shard_map/exchange/pallas_call | solution.py:261
  158.5 0.0 copy-start
  158.5 0.8 copy-done
  159.3 0.0 copy-start.1
  159.3 0.7 copy-done.1
  160.0 1.7 %reshape.119 = bf16[8,14336]{1,0:T(8,128)(2,1)} reshape(bf16[128,896]{1,0:T(8,128)(2,1)} %copy-done.1) | data formatting | bytes 458752 | tf_op jit(solution)/shard_map/reshape | solution.py:469
  161.7 1.9 %copy.20 = bf16[512,512]{1,0:T(8,128)(2,1)} copy(bf16[512,512]{1,0:T(8,128)(2,1)} %copy-done) | data formatting | bytes 1048576
  163.6 0.8 copy.21
  (5 shorter events, 0.0 us)
Async XLA Ops:
  0.6 2.6 %copy-start.3 = (bf16[896,512]{1,0:T(8,128)(2,1)S(1)}, bf16[896,512]{1,0:T(8,128)(2,1)}, u32[]{:S(2)}) copy-start(bf16[896,512]{1,0:T(8,128)(2,1)} %param.13) | copy-start | bytes 2752516
  1.8 1.8 %copy-start.2 = (bf16[8,114688]{1,0:T(8,128)(2,1)S(1)}, bf16[8,114688]{1,0:T(8,128)(2,1)}, u32[]{:S(2)}) copy-start(bf16[8,114688]{1,0:T(8,128)(2,1)} %param.9) | copy-start | bytes 5505028
  158.5 0.8 copy-start
  159.3 0.7 copy-start.1

commit v6 on v5

--- a/solution.py
+++ b/solution.py
@@ -139,7 +139,7 @@
 
 
 def exchange_kernel(
-    n, owners, stored, attn, gq, w_out_hbm, w_query_hbm, w_pair, outgoing, sent_ids,
+    n, owners, stored, attn, gq, w_out_hbm, w_query_hbm, w_key, w_value, outgoing, sent_ids,
     att_out, hid_out, enc_out, w_out, w_query, load_sem, returned, returned_ids,
     att_buf, hid_buf, enc_buf, att_first, hid_first, enc_first,
     att_send, att_recv, hid_send, hid_recv, enc_send, enc_recv,
@@ -207,7 +207,9 @@
             block_rows = returned[q * rows:(q + 1) * rows, pl.ds(base, window), :]
             term = dot(hit, block_rows.reshape(rows * window, -1), (1, 0))
             total = term if total is None else total + term
-        return dot(total.astype(jnp.bfloat16), w_pair[...], (1, 1))
+        total = total.astype(jnp.bfloat16)
+        cols = w_key.shape[1]
+        return dot(total[:, :cols], w_key[...], (1, 1)) + dot(total[:, cols:], w_value[...], (1, 1))
 
     att = Ring(n, ahead, chunk, lambda c: dot(attn[...], w_out[:, at(c)], (1, 0)),
                att_buf, att_first, att_send, att_recv, att_out)
@@ -249,18 +251,18 @@
         ring.drain()
 
 
-def exchange(attn, gq, w_out, w_query, w_pair, outgoing, sent_ids, stored):
+def exchange(attn, gq, w_out, w_query, w_key, w_value, outgoing, sent_ids, stored):
     n, owners = lax.axis_size("mp"), lax.axis_size("dp")
     tok = attn.shape[0]
     width = w_out.shape[1] // n
     vmem = pl.BlockSpec(memory_space=pltpu.VMEM)
     anywhere = pl.BlockSpec(memory_space=pl.ANY)
-    shapes = [(tok, width), (tok, width), (stored * outgoing.shape[1] // n, w_pair.shape[0])]
+    shapes = [(tok, width), (tok, width), (stored * outgoing.shape[1] // n, w_key.shape[0])]
     ring = pltpu.SemaphoreType.DMA((n - 1,))
     peers = pltpu.SemaphoreType.DMA((owners - 1,))
     return pl.pallas_call(
         functools.partial(exchange_kernel, n, owners, stored),
-        in_specs=[vmem] * 2 + [anywhere] * 2 + [vmem] + [anywhere] * 2,
+        in_specs=[vmem] * 2 + [anywhere] * 2 + [vmem] * 2 + [anywhere] * 2,
         out_specs=[vmem] * 3,
         out_shape=[jax.ShapeDtypeStruct(shape, jnp.bfloat16) for shape in shapes],
         scratch_shapes=[pltpu.VMEM(w.shape, w.dtype) for w in (w_out, w_query)]
@@ -275,11 +277,11 @@
             collective_id=1, has_side_effects=True, vmem_limit_bytes=VMEM_BYTES
         ),
         name="exchange",
-    )(attn, gq, w_out, w_query, w_pair, outgoing, sent_ids)
+    )(attn, gq, w_out, w_query, w_key, w_value, outgoing, sent_ids)
 
 
 def fetch_kernel(
-    nx, rows, hidden, w_query, cotangent, w_out, w_pair, queries, grad_attn, kv,
+    nx, rows, hidden, w_query, cotangent, w_out, w_key, w_value, queries, grad_attn, kv,
     held, hid_v, wq_v, cot_v, wo_v,
     load_sem, x_send, x_recv, y_send, y_recv, own_send, own_recv,
     cx_send, cx_recv, cy_send, cy_recv,
@@ -329,8 +331,11 @@
 
     def project(src, first, place):
         block = src[pl.ds(first, half)].reshape(half * seg, width)
-        out = dot(block, w_pair[...], (1, 0)).astype(jnp.bfloat16)
-        kv[pl.ds(place, half)] = out.reshape(half, seg, -1)
+        cols = w_key.shape[1]
+        keys = dot(block, w_key[...], (1, 0)).astype(jnp.bfloat16)
+        kv[pl.ds(place, half), :, :cols] = keys.reshape(half, seg, -1)
+        values = dot(block, w_value[...], (1, 0)).astype(jnp.bfloat16)
+        kv[pl.ds(place, half), :, cols:] = values.reshape(half, seg, -1)
 
     y_copies, cx_copies, cy_copies = [], [], []
 
@@ -404,7 +409,7 @@
         copy.wait_send()
 
 
-def fetch(rows, hidden, w_query, cotangent, w_out, w_pair):
+def fetch(rows, hidden, w_query, cotangent, w_out, w_key, w_value):
     owners = lax.axis_size("dp")
     nx = owners // 2
     stored, seg, _ = rows.shape
@@ -414,12 +419,12 @@
     pieces = pltpu.SemaphoreType.DMA(((nx - 1) * stored // 2,))
     return pl.pallas_call(
         functools.partial(fetch_kernel, nx),
-        in_specs=[vmem] + [anywhere] * 4 + [vmem],
+        in_specs=[vmem] + [anywhere] * 4 + [vmem] * 2,
         out_specs=[vmem] * 3,
         out_shape=[
             jax.ShapeDtypeStruct((tok, cols), jnp.bfloat16),
             jax.ShapeDtypeStruct((tok, cols), jnp.bfloat16),
-            jax.ShapeDtypeStruct((owners * stored, seg, w_pair.shape[1]), jnp.bfloat16),
+            jax.ShapeDtypeStruct((owners * stored, seg, 2 * w_key.shape[1]), jnp.bfloat16),
         ],
         scratch_shapes=[pltpu.VMEM((owners * stored,) + rows.shape[1:], jnp.bfloat16)]
         + [pltpu.VMEM(a.shape, a.dtype) for a in (hidden, w_query, cotangent, w_out)]
@@ -431,7 +436,7 @@
             collective_id=3, has_side_effects=True, vmem_limit_bytes=VMEM_BYTES
         ),
         name="fetch",
-    )(rows, hidden, w_query, cotangent, w_out, w_pair)
+    )(rows, hidden, w_query, cotangent, w_out, w_key, w_value)
 
 
 def shards(hidden, encoded, neighbours, w_query, w_key, w_value, w_out, cotangent):
@@ -443,9 +448,8 @@
     enc_width, head_cols = w_key.shape
     seg_len = encoded.shape[1] // enc_width
 
-    w_pair = jnp.concatenate([w_key, w_value], axis=1)
     queries, grad_attn, kv = fetch(
-        encoded.reshape(stored, seg_len, enc_width), hidden, w_query, cotangent, w_out, w_pair
+        encoded.reshape(stored, seg_len, enc_width), hidden, w_query, cotangent, w_out, w_key, w_value
     )
     flat_ids = neighbours.reshape(requests)
     flat_owner = flat_ids // stored
@@ -464,7 +468,7 @@
         flat_ids, target, queries, grad_attn, kv, blocks, owners * capacity
     )
     attended, grad_hidden, grad_encoded = exchange(
-        attn, grad_query, w_out, w_query, w_pair, outgoing, sent_ids, stored
+        attn, grad_query, w_out, w_query, w_key, w_value, outgoing, sent_ids, stored
     )
     return attended, grad_hidden, grad_encoded.reshape(stored, -1)
 

time: 165 us -> 165 us (level)
    unnamed x13 -> x12, local copies, waits for them, and re-layouts: 6.89 us -> 6.82 us
where the time goes in v6:
time: 165 us; the launch traced here: 164 us
  Pallas kernels  154 us (93%)
  local copies, waits for them, and re-layouts  8.89 us (5%)
    pallas_call x1, Pallas kernels, exchange(): pl.pallas_call(functools.partial(exchange_kernel, n, owners, stored), in_...  107 us
    pallas_call x1, Pallas kernels, fetch(): pl.pallas_call(functools.partial(fetch_kernel, nx), in_specs=[vmem] + [an...  36.9 us
    pallas_call x1, Pallas kernels, attention(): pl.pallas_call(functools.partial(attention_kernel, per_block), grid_spec=...  10.8 us
    unnamed x12, local copies, waits for them, and re-layouts  6.82 us

profile of v6, /device:TPU:0, one launch (start us, length us, event | category | flops | bytes accessed | tf_op | source)
XLA Modules:
  0.0 164.2 jit_solution(7808975822138924804)
XLA Ops:
  0.6 0.0 copy-start
  0.6 0.0 copy-start.1
  0.7 0.9 copy.13
  1.5 0.1 reshape.117.ids
  1.6 0.2 convert_reduce_fusion
  1.8 1.8 %copy.16 = bf16[1,8,128,896]{3,2,1,0:T(8,128)(2,1)S(1)} copy(bf16[1,8,128,896]{3,1,2,0:T(8,128)(2,1)} %bitcast.5) | data formatting | bytes 3670016
  3.6 0.0 copy-done
  3.6 0.0 copy-done.1
  3.6 36.9 %fetch.1 = (bf16[512,512]{1,0:T(8,128)(2,1)S(1)}, bf16[512,512]{1,0:T(8,128)(2,1)S(1)}, bf16[32,128,1024]{2,1,0:T(8,128)(2,1)}) custom-call(bf16[8,128,896]{2,1,0:T(8,128)(2,1)S(1)} %bitcast.4, bf16[512,4096]{1,0:T(8,128)(2,1)} %hidden.1, bf16[4096,512]{1,0:T(8,128)(2,1)} %w_query_hbm.1, bf16[512,4096]{1,0:T(8,128)(2,1)} %cotangent.1, ...), custom_call_target="tpu_custom_call" | custom-call | tf_op jit(solution)/shard_map/fetch/pallas_call | solution.py:420
  40.5 10.8 %attention.1 = (bf16[512,512]{1,0:T(8,128)(2,1)S(1)}, bf16[512,512]{1,0:T(8,128)(2,1)S(1)}, bf16[16,128,1024]{2,1,0:T(8,128)(2,1)}) custom-call(s32[16]{0:T(128)S(1)} %reshape.117.ids, s32[16]{0:T(128)S(1)} %multiply_add_fusion.target, bf16[512,512]{1,0:T(8,128)(2,1)S(1)} %get-tuple-element.12.q_ref, bf16[512,512]{1,0:T(8,128)(2,1)S(1)} %get-tuple-element.13.ga_ref, ...), custom_call_target="tpu_custom_call" | custom-call | tf_op jit(solution)/shard_map/attention/pallas_call | solution.py:66
  51.3 0.1 select_reduce_fusion
  51.4 0.1 sub.11
  51.5 0.1 broadcast_in_dim.31
  51.6 0.1 broadcast_in_dim.32
  51.7 106.6 %exchange.1 = (bf16[512,512]{1,0:T(8,128)(2,1)S(1)}, bf16[512,512]{1,0:T(8,128)(2,1)S(1)}, bf16[128,896]{1,0:T(8,128)(2,1)S(1)}) custom-call(bf16[512,512]{1,0:T(8,128)(2,1)S(1)} %get-tuple-element.15.attn, bf16[512,512]{1,0:T(8,128)(2,1)S(1)} %get-tuple-element.16.gq, bf16[512,4096]{1,0:T(8,128)(2,1)} %w_out_hbm.1, bf16[4096,512]{1,0:T(8,128)(2,1)} %w_query_hbm.1, ...), custom_call_target="tpu_custom_call" | custom-call | tf_op jit(solution)/shard_map/exchange/pallas_call | solution.py:263
  158.3 0.0 copy-start.2
  158.4 0.8 copy-done.2
  159.1 0.0 copy-start.3
  159.1 0.7 copy-done.3
  159.8 1.7 %reshape.119 = bf16[8,14336]{1,0:T(8,128)(2,1)} reshape(bf16[128,896]{1,0:T(8,128)(2,1)} %copy-done.3) | data formatting | bytes 458752 | tf_op jit(solution)/shard_map/reshape | solution.py:473
  161.6 1.9 %copy.19 = bf16[512,512]{1,0:T(8,128)(2,1)} copy(bf16[512,512]{1,0:T(8,128)(2,1)} %copy-done.2) | data formatting | bytes 1048576
  163.4 0.8 copy.20
  (5 shorter events, 0.0 us)
Async XLA Ops:
  0.6 3.0 %copy-start = (bf16[896,512]{1,0:T(8,128)(2,1)S(1)}, bf16[896,512]{1,0:T(8,128)(2,1)}, u32[]{:S(2)}) copy-start(bf16[896,512]{1,0:T(8,128)(2,1)} %w_key.3) | copy-start | bytes 2752516
  0.6 3.0 %copy-start.1 = (bf16[896,512]{1,0:T(8,128)(2,1)S(1)}, bf16[896,512]{1,0:T(8,128)(2,1)}, u32[]{:S(2)}) copy-start(bf16[896,512]{1,0:T(8,128)(2,1)} %w_value.3) | copy-start | bytes 2752516
  158.3 0.8 copy-start.2
  159.1 0.7 copy-start.3
